TPU v7x, 256 devices: a whole 4x4x8 slice. The times are simulated.
256 devices in a mesh: gz: 64 (over y, z, core), xy: 4 (over x).
Axes of the slice: x: 4, y: 4, z: 8, core: 2. Of those that a mesh axis runs over, the one named last changes fastest.
Arguments:
- sections: bfloat16 [256, 512, 2048], P('gz', 'xy'), may hold values from -16 to 16
- skips: int32 [256, 2], P('gz'), may hold values from 0 to 3, as said below
- patch_valid: int32 [256, 8, 32], P('gz', 'xy'), may hold values 0 or 1
- velocity_start: float32 [256, 2, 8, 32], P('gz', None, 'xy'), may hold values from -8 to 8
- step_size: float32 [3], replicated, may hold values from 0.15 to 0.45
- mixing: float32 [3], replicated, may hold values from 0.1 to 0.6
Outputs:
- flow_field: float32 [256, 2, 2, 8, 32], P('gz', None, None, 'xy')
- displace: float32 [256, 2, 8, 32], P('gz', None, 'xy')
Inputs may be any that keep to these rules, and one draw needn't show every extreme that they name: `skips`: entry 0 of a row is the first partner's distance, 1 to 3; entry 1 is 0 where there is no second partner, else a distance of 1 to 3 other than entry 0. Some row has distance 3.
All inputs are finite; a program needn't handle non-finite values. No bound on the sum of `patch_valid` on one device may be relied on, other than what follows from the above.
Results may differ from a plain program's by a relative error of at most 0.0014.
Values may be sent and summed in bfloat16 or wider, within the bound.
A program may use at most 128 MiB of HBM per device.

v0:
```python
import jax
import jax.numpy as jnp
from jax import lax
from jax.sharding import PartitionSpec as P

PATCH = 64
REACH = 3
ITERS = 3


SHARP = 400.0
STIFF = 0.25
TINY = 1e-06


def passed_along(x, axis, by):
    length = lax.axis_size(axis)
    pairs = [(i, i + by) for i in range(length) if 0 <= i + by < length]
    return lax.ppermute(x, axis, pairs)


def with_halo(cells, sides, width):
    for axis, dim in sides:
        count = lax.axis_size(axis)
        ends = count - 1
        head = lax.slice_in_dim(cells, 0, width, axis=dim)
        tail = lax.slice_in_dim(cells, cells.shape[dim] - width, cells.shape[dim], axis=dim)
        cells = jnp.concatenate(
            [
                lax.ppermute(tail, axis, [(i, (i + 1) % count) for i in range(ends)]),
                cells,
                lax.ppermute(head, axis, [((i + 1) % count, i) for i in range(ends)]),
            ],
            axis=dim,
        )
    return cells


def tables():
    indices = jnp.arange(PATCH, dtype=jnp.int32)
    phases = indices[:, None] * indices[None, :] % PATCH
    angles = phases.astype(jnp.float32) * (2.0 * jnp.pi / PATCH)
    cosine = jnp.cos(angles)
    sines = jnp.sin(angles)
    forward_cols = jnp.concatenate([cosine, sines], axis=1).astype(jnp.bfloat16)
    forward_rows = jnp.concatenate([cosine, sines], axis=0).astype(jnp.bfloat16)
    inverse_cols = jnp.concatenate(
        [jnp.concatenate([cosine, sines], axis=1), jnp.concatenate([-sines, cosine], axis=1)],
        axis=0,
    ).astype(jnp.bfloat16)
    inverse_rows = jnp.stack([cosine, -sines], axis=1).astype(jnp.bfloat16)
    shifts = jnp.where(indices < PATCH // 2, indices, indices - PATCH).astype(jnp.float32)
    return (forward_cols, forward_rows, inverse_cols, inverse_rows, shifts)


def spectra(image_tile, forward_cols, forward_rows):
    patch_rows = image_tile.shape[0] // PATCH
    patch_cols = image_tile.shape[1] // PATCH
    blocks = image_tile.astype(jnp.float32).reshape(patch_rows, PATCH, patch_cols, PATCH)
    centred = blocks - jnp.mean(blocks, axis=(1, 3), keepdims=True)
    spread = jnp.mean(centred * centred, axis=(1, 3), keepdims=True)
    normed = (centred * lax.rsqrt(spread + 1e-05)).astype(jnp.bfloat16)
    halfway = jnp.einsum(
        "anbm,mc->anbc", normed, forward_cols, preferred_element_type=jnp.float32
    ).astype(jnp.bfloat16)
    combined = jnp.einsum(
        "kn,anbc->abkc", forward_rows, halfway, preferred_element_type=jnp.float32
    )
    cos_part = combined[:, :, :PATCH, :]
    sin_part = combined[:, :, PATCH:, :]
    real_part = cos_part[..., :PATCH] - sin_part[..., PATCH:]
    imag_part = -(sin_part[..., :PATCH] + cos_part[..., PATCH:])
    return jnp.concatenate([real_part, imag_part], axis=-1).astype(jnp.bfloat16)


def soft_flow(spec_self, partners, inverse_cols, inverse_rows, shifts):
    spec_mine = spec_self.astype(jnp.float32)[:, :, :, None, :]
    spec_other = partners.astype(jnp.float32)
    real_self = spec_mine[..., :PATCH]
    imag_self = spec_mine[..., PATCH:]
    real_other = spec_other[..., :PATCH]
    imag_other = spec_other[..., PATCH:]
    cross_spec = jnp.concatenate(
        [
            real_self * real_other + imag_self * imag_other,
            real_self * imag_other - imag_self * real_other,
        ],
        axis=-1,
    ).astype(jnp.bfloat16)
    inverse_half = jnp.einsum(
        "abkjc,cd->abkjd", cross_spec, inverse_cols, preferred_element_type=jnp.float32
    ).astype(jnp.bfloat16)
    shape_now = inverse_half.shape
    inverse_half = inverse_half.reshape(shape_now[0], shape_now[1], PATCH, shape_now[3], 2, PATCH)
    correlation = jnp.einsum(
        "trk,abkjrc->abtjc", inverse_rows, inverse_half, preferred_element_type=jnp.float32
    )
    scores = correlation * (SHARP / float(PATCH**4))
    peak_score = jnp.max(scores, axis=(2, 4), keepdims=True)
    soft_weights = jnp.exp(scores - peak_score)
    total_sum = jnp.sum(soft_weights, axis=(2, 4))
    along_rows = jnp.sum(soft_weights * shifts[None, None, :, None, None], axis=(2, 4)) / total_sum
    along_cols = jnp.sum(soft_weights * shifts[None, None, None, None, :], axis=(2, 4)) / total_sum
    return jnp.transpose(jnp.stack([along_rows, along_cols], axis=0), (3, 0, 1, 2))


def body(sections, skips, patch_valid, velocity_start, step_size, mixing):
    forward_cols, forward_rows, inverse_cols, inverse_rows, shifts = tables()
    sections_here = sections.shape[0]
    patch_rows = sections.shape[1] // PATCH
    patch_cols = sections.shape[2] // PATCH
    first_index = lax.axis_index("gz") * sections_here
    all_sections = sections_here * lax.axis_size("gz")
    valid_bf = patch_valid.astype(jnp.bfloat16)

    def section_spectra(image_tile):
        return spectra(image_tile, forward_cols, forward_rows)

    own_spec = lax.map(section_spectra, sections)
    far_spec, far_valid = passed_along((own_spec[:REACH], valid_bf[:REACH]), "gz", -1)
    ext_spec = jnp.concatenate([own_spec, far_spec], axis=0)
    ext_valid = jnp.concatenate([valid_bf, far_valid], axis=0).astype(jnp.float32)
    positions = jnp.arange(sections_here, dtype=jnp.int32)
    target = positions[:, None] + skips
    paired = (skips > 0) & (first_index + target < all_sections)

    def pair_flow(section_item):
        spec_self, target_row = section_item
        partners = jnp.stack([ext_spec[target_row[0]], ext_spec[target_row[1]]], axis=3)
        return soft_flow(spec_self, partners, inverse_cols, inverse_rows, shifts)

    flow_field = lax.map(pair_flow, (own_spec, target))
    flow_field = jnp.where(paired[:, :, None, None, None], flow_field, 0.0)
    valid_mask = patch_valid.astype(jnp.float32)
    weight = paired.astype(jnp.float32)[:, :, None, None] * valid_mask[:, None] * ext_valid[target]
    select = (
        target.T[:, :, None] == jnp.arange(sections_here + REACH, dtype=jnp.int32)[None, None, :]
    ).astype(jnp.float32)
    displace = jnp.zeros((sections_here, 2, patch_rows, patch_cols), jnp.float32)
    velocity = velocity_start
    for iteration in range(ITERS):
        padded = with_halo(displace, (("xy", 2),), 1)
        padded = jnp.pad(padded, ((0, 0), (0, 0), (0, 0), (1, 1)))
        far_mesh = passed_along(displace[:REACH], "gz", -1)
        ext_mesh = jnp.concatenate([displace, far_mesh], axis=0)
        partner = jnp.einsum("jsq,qcab->sjcab", select, ext_mesh, precision=lax.Precision.HIGHEST)
        tension = weight[:, :, None] * (partner - displace[:, None] - flow_field)
        pushed = jnp.einsum("jsq,sjcab->qcab", select, tension, precision=lax.Precision.HIGHEST)
        arrived = passed_along(pushed[sections_here:], "gz", 1)
        incoming = jnp.pad(arrived, ((0, sections_here - REACH), (0, 0), (0, 0), (0, 0)))
        forces = STIFF * (
            padded[:, :, 2:, 1:-1]
            + padded[:, :, :-2, 1:-1]
            + padded[:, :, 1:-1, 2:]
            + padded[:, :, 1:-1, :-2]
            - 4.0 * displace
        ) + (jnp.sum(tension, axis=1) - pushed[:sections_here] - incoming)
        power_sum, speed_sum, strength = lax.psum(
            (jnp.sum(forces * velocity), jnp.sum(velocity * velocity), jnp.sum(forces * forces)),
            ("gz", "xy"),
        )
        gating = 0.5 + 0.5 * power_sum / jnp.sqrt((speed_sum + TINY) * (strength + TINY))
        scale_ratio = jnp.sqrt((speed_sum + TINY) / (strength + TINY))
        velocity = gating * (
            (1.0 - mixing[iteration]) * velocity + mixing[iteration] * scale_ratio * forces
        )
        velocity = velocity + step_size[iteration] * forces
        displace = displace + step_size[iteration] * velocity
    return (flow_field, displace)


def solution(mesh):
    in_specs = (
        P("gz", "xy", None),
        P("gz", None),
        P("gz", "xy", None),
        P("gz", None, "xy", None),
        P(),
        P(),
    )
    out_specs = (P("gz", None, None, "xy", None), P("gz", None, "xy", None))
    return jax.shard_map(body, mesh=mesh, in_specs=in_specs, out_specs=out_specs, check_vma=False)
```

profile of v0, /device:TPU:1, one launch (start us, length us, event | category | flops | bytes accessed | tf_op | source)
XLA Modules:
  0.0 472.8 jit_solution(12844769580796416977)
XLA Ops:
  1.1 57.7 %while.24 = (s32[]{:T(128)}, bf16[4,2,32,64,128]{4,3,2,1,0:T(8,128)(2,1)}, bf16[4,128,2048]{2,1,0:T(8,128)(2,1)}, bf16[64,128]{1,0:T(8,128)(2,1)S(1)}, bf16[128,64]{0,1:T(8,128)(2,1)S(1)}) while((s32[]{:T(128)}, bf16[4,2,32,64,128]{4,3,2,1,0:T(8,128)(2,1)}, bf16[4,128,2048]{2,1,0:T(8,128)(2,1)}, bf16[64,128]{1,0:T(8,128)(2,1)S(1)}, ...), condition=%wide.region_3.4_spmd.clone, body=%wide.region_0.3_spmd.sunk.clone | while | flops 207355968 | bytes 18385732 | solution.py:119
  3.4 2.0 multiply_reduce_fusion.16
  5.4 3.9 convolution_bitcast_fusion.9
  9.3 4.7 fusion.126
  14.0 1.6 maximum_dynamic-update-slice_fusion.3
  17.8 2.0 multiply_reduce_fusion.16
  19.8 3.9 convolution_bitcast_fusion.9
  23.7 4.7 fusion.126
  28.4 1.7 maximum_dynamic-update-slice_fusion.3
  32.3 2.0 multiply_reduce_fusion.16
  34.3 3.9 convolution_bitcast_fusion.9
  38.2 4.7 fusion.126
  42.9 1.6 maximum_dynamic-update-slice_fusion.3
  46.7 2.0 multiply_reduce_fusion.16
  48.7 3.9 convolution_bitcast_fusion.9
  52.6 4.7 fusion.126
  57.3 1.6 maximum_dynamic-update-slice_fusion.3
  58.9 4.8 %slice.155 = bf16[3,2,32,64,128]{4,3,2,1,0:T(8,128)(2,1)} slice(bf16[4,2,32,64,128]{4,3,2,1,0:T(8,128)(2,1)} %get-tuple-element.423), slice={[0:3], [0:2], [0:32], [0:64], [0:128]} | slice | bytes 6291456 | tf_op jit(solution)/shard_map/slice | solution.py:120
  63.6 5.1 %collective-permute-start = (bf16[3,2,32,64,128]{4,3,2,1,0:T(8,128)(2,1)}, bf16[3,2,32,64,128]{4,3,2,1,0:T(8,128)(2,1)S(1)}, u32[]{:S(2)}, u32[]{:S(2)}) collective-permute-start(bf16[3,2,32,64,128]{4,3,2,1,0:T(8,128)(2,1)} %slice.155), channel_id=1, source_target_pairs={{4,0},{8,4},{12,8},{16,12},{20,16},{24,20},{28,24},{32,28},{36,32}... | collective-permute-start | bytes 9437192 | tf_op jit(solution)/shard_map/ppermute | solution.py:19
  68.8 1.3 collective-permute-start.1
  70.1 4.0 collective-permute-start.2
  74.1 1.9 collective-permute-start.3
  76.1 2.1 collective-permute-start.4
  82.7 21.0 %collective-permute-done.3 = bf16[3,2,32]{2,1,0:T(2,128)(2,1)S(1)} collective-permute-done((bf16[3,2,32]{2,1,0:T(2,128)(2,1)S(1)}, bf16[3,2,32]{2,1,0:T(2,128)(2,1)S(1)}, u32[]{:S(2)}, u32[]{:S(2)}) %collective-permute-start.3) | collective-permute-done | bytes 416 | tf_op jit(solution)/shard_map/ppermute | solution.py:19
  104.4 5.8 %pad_maximum_fusion.1 = bf16[7,2,32,64,128]{4,3,2,1,0:T(8,128)(2,1)} fusion(bf16[3,2,32,64,128]{4,3,2,1,0:T(8,128)(2,1)S(1)} %collective-permute-done, bf16[4,2,32,64,128]{4,3,2,1,0:T(8,128)(2,1)} %get-tuple-element.423), kind=kLoop, calls=%fused_computation.50 | loop fusion | flops 3670016 | bytes 14680064 | tf_op jit(solution)/shard_map/concatenate | solution.py:121
  110.2 85.6 %while.25 = (s32[]{:T(128)}, f32[4,2,2,2,32]{4,0,1,3,2:T(4,128)S(1)}, bf16[4,2,32,64,128]{4,3,2,1,0:T(8,128)(2,1)}, s32[4,2]{0,1:T(2,128)S(1)}, bf16[7,2,32,64,1...) while((s32[]{:T(128)}, ...), condition=%wide.region_9.10_spmd.clone.clone.clone, body=%wide.region_4.9_spmd.clone.clone.sunk.clone | while | flops 419430656 | bytes 40955588 | solution.py:132
  114.6 1.7 dynamic-slice_bitcast_fusion.4
  116.6 1.5 bitcast_convert_fusion.3
  118.9 2.0 add_convert_fusion.3
  120.9 1.3 fusion.131
  122.2 3.2 copy.103
  125.4 3.5 bitcast_reduce_fusion.3
  129.0 2.4 multiply_reduce_fusion.17
  136.0 1.7 dynamic-slice_bitcast_fusion.4
  138.0 1.5 bitcast_convert_fusion.3
  140.3 2.0 add_convert_fusion.3
  142.3 1.3 fusion.131
  143.6 3.2 copy.103
  146.8 3.5 bitcast_reduce_fusion.3
  150.4 2.4 multiply_reduce_fusion.17
  157.4 1.7 dynamic-slice_bitcast_fusion.4
  159.4 1.5 bitcast_convert_fusion.3
  161.7 2.0 add_convert_fusion.3
  165.0 3.2 copy.103
  168.2 3.5 bitcast_reduce_fusion.3
  171.8 2.4 multiply_reduce_fusion.17
  178.8 1.7 dynamic-slice_bitcast_fusion.4
  180.8 1.5 bitcast_convert_fusion.3
  183.1 2.0 add_convert_fusion.3
  186.4 3.2 copy.103
  189.6 3.5 bitcast_reduce_fusion.3
  193.2 2.4 multiply_reduce_fusion.17
  196.4 1.9 collective-permute-start.5
  200.2 81.5 %all-reduce.11 = (f32[]{:T(128)}, f32[]{:T(128)}, f32[]{:T(128)}) all-reduce(f32[]{:T(128)} %multiply_reduce_fusion.10, f32[]{:T(128)} %get-tuple-element.164, f32[]{:T(128)} %get-tuple-element.163), channel_id=1, replica_groups=mesh['gz'=64,'xy'=4] {'gz','xy'}, use_global_device_ids=true, to_apply=%region_14.15 | all-reduce | flops 3 | bytes 24 | tf_op jit(solution)/shard_map/psum | solution.py:158
  285.0 2.6 collective-permute-start.8
  287.6 1.3 collective-permute-start.6
  288.9 4.0 collective-permute-start.7
  293.4 4.1 collective-permute-start.9
  299.1 76.3 %all-reduce.10 = (f32[]{:T(128)}, f32[]{:T(128)}, f32[]{:T(128)}) all-reduce(f32[]{:T(128)} %get-tuple-element.161, f32[]{:T(128)} %get-tuple-element.162, f32[]{:T(128)} %get-tuple-element.160), channel_id=1, replica_groups=mesh['gz'=64,'xy'=4] {'gz','xy'}, use_global_device_ids=true, to_apply=%region_21.22 | all-reduce | flops 3 | bytes 24 | tf_op jit(solution)/shard_map/psum | solution.py:158
  378.6 2.6 collective-permute-start.12
  381.2 1.3 collective-permute-start.10
  382.5 4.0 collective-permute-start.11
  387.0 4.1 collective-permute-start.13
  392.7 76.2 %all-reduce.9 = (f32[]{:T(128)}, f32[]{:T(128)}, f32[]{:T(128)}) all-reduce(f32[]{:T(128)} %get-tuple-element.158, f32[]{:T(128)} %get-tuple-element.159, f32[]{:T(128)} %get-tuple-element.157), channel_id=1, replica_groups=mesh['gz'=64,'xy'=4] {'gz','xy'}, use_global_device_ids=true, to_apply=%region_28.29 | all-reduce | flops 3 | bytes 24 | tf_op jit(solution)/shard_map/psum | solution.py:158
  (137 shorter events, 32.2 us)
Async XLA Ops:
  58.9 15.2 %copy-start.3 = (s32[4,2,32]{2,1,0:T(2,128)S(1)}, s32[4,2,32]{2,1,0:T(2,128)}, u32[]{:S(2)}) copy-start(s32[4,2,32]{2,1,0:T(2,128)} %param.12) | copy-start | bytes 3076
  58.9 19.3 %copy-start.4 = (s32[4,2]{0,1:T(2,128)S(1)}, s32[4,2]{0,1:T(2,128)}, u32[]{:S(2)}) copy-start(s32[4,2]{0,1:T(2,128)} %param.11) | copy-start | bytes 100
  58.9 19.5 %copy-start.1 = (f32[3]{0:T(128)S(1)}, f32[3]{0:T(128)}, u32[]{:S(2)}) copy-start(f32[3]{0:T(128)} %param.15) | copy-start | bytes 40
  58.9 20.8 %copy-start.2 = (f32[3]{0:T(128)S(1)}, f32[3]{0:T(128)}, u32[]{:S(2)}) copy-start(f32[3]{0:T(128)} %param.14) | copy-start | bytes 40
  58.9 21.7 %copy-start = (f32[4,2,2,32]{3,2,1,0:T(2,128)S(1)}, f32[4,2,2,32]{3,2,1,0:T(2,128)}, u32[]{:S(2)}) copy-start(f32[4,2,2,32]{3,2,1,0:T(2,128)} %param.13) | copy-start | bytes 6148
  63.6 40.8 %collective-permute-start = (bf16[3,2,32,64,128]{4,3,2,1,0:T(8,128)(2,1)}, bf16[3,2,32,64,128]{4,3,2,1,0:T(8,128)(2,1)S(1)}, u32[]{:S(2)}, u32[]{:S(2)}) collective-permute-start(bf16[3,2,32,64,128]{4,3,2,1,0:T(8,128)(2,1)} %slice.155), channel_id=1, source_target_pairs={{4,0},{8,4},{12,8},{16,12},{20,16},{24,20},{28,24},{32,28},{36,32}... | collective-permute-start | bytes 9437192 | tf_op jit(solution)/shard_map/ppermute | solution.py:19
  68.8 129.5 %collective-permute-start.1 = (f32[4,2,1,32]{3,0,2,1:T(4,128)S(1)}, f32[4,2,1,32]{3,0,2,1:T(4,128)S(1)}, u32[]{:S(2)}, u32[]{:S(2)}) collective-permute-start(f32[4,2,1,32]{3,0,2,1:T(4,128)S(1)} %broadcast.179), channel_id=1, source_target_pairs={{1,0},{2,1},{3,2},{5,4},{6,5},{7,6},{9,8},{10,9},{11,10},{13,12},{... | collective-permute-start | bytes 3080 | tf_op jit(solution)/shard_map/ppermute | solution.py:32
  70.1 128.3 %collective-permute-start.2 = (f32[4,2,1,32]{3,0,2,1:T(4,128)S(1)}, f32[4,2,1,32]{3,0,2,1:T(4,128)S(1)}, u32[]{:S(2)}, u32[]{:S(2)}) collective-permute-start(f32[4,2,1,32]{3,0,2,1:T(4,128)S(1)} %broadcast.179), channel_id=1, source_target_pairs={{0,1},{1,2},{2,3},{4,5},{5,6},{6,7},{8,9},{9,10},{10,11},{12,13},{... | collective-permute-start | bytes 3080 | tf_op jit(solution)/shard_map/ppermute | solution.py:30
  74.1 29.6 %collective-permute-start.3 = (bf16[3,2,32]{2,1,0:T(2,128)(2,1)S(1)}, bf16[3,2,32]{2,1,0:T(2,128)(2,1)S(1)}, u32[]{:S(2)}, u32[]{:S(2)}) collective-permute-start(bf16[3,2,32]{2,1,0:T(2,128)(2,1)S(1)} %slice.210), channel_id=1, source_target_pairs={{4,0},{8,4},{12,8},{16,12},{20,16},{24,20},{28,24},{32,28},{36,32}... | collective-permute-start | bytes 1160 | tf_op jit(solution)/shard_map/ppermute | solution.py:19
  76.1 119.8 %collective-permute-start.4 = (f32[3,2,2,32]{3,0,2,1:T(4,128)S(1)}, f32[3,2,2,32]{3,0,2,1:T(4,128)S(1)}, u32[]{:S(2)}, u32[]{:S(2)}) collective-permute-start(f32[3,2,2,32]{3,0,2,1:T(4,128)S(1)} %slice.162), channel_id=1, source_target_pairs={{4,0},{8,4},{12,8},{16,12},{20,16},{24,20},{28,24},{32,28},{36,32}... | collective-permute-start | bytes 4616 | tf_op jit(solution)/shard_map/ppermute | solution.py:19
  196.4 3.1 collective-permute-start.5
  285.0 7.9 %collective-permute-start.8 = (f32[3,2,2,32]{3,0,2,1:T(4,128)S(1)}, f32[3,2,2,32]{3,0,2,1:T(4,128)S(1)}, u32[]{:S(2)}, u32[]{:S(2)}) collective-permute-start(f32[3,2,2,32]{3,0,2,1:T(4,128)S(1)} %bitcast.233), channel_id=1, source_target_pairs={{4,0},{8,4},{12,8},{16,12},{20,16},{24,20},{28,24},{32,28},{36,32}... | collective-permute-start | bytes 4616 | tf_op jit(solution)/shard_map/ppermute | solution.py:19
  287.6 10.0 %collective-permute-start.6 = (f32[4,2,1,32]{3,0,2,1:T(4,128)S(1)}, f32[4,2,1,32]{3,0,2,1:T(4,128)S(1)}, u32[]{:S(2)}, u32[]{:S(2)}) collective-permute-start(f32[4,2,1,32]{3,0,2,1:T(4,128)S(1)} %get-tuple-element.224), channel_id=1, source_target_pairs={{1,0},{2,1},{3,2},{5,4},{6,5},{7,6},{9,8},{10,9},{11,10},{13,12},{... | collective-permute-start | bytes 3080 | tf_op jit(solution)/shard_map/ppermute | solution.py:32
  288.9 8.7 %collective-permute-start.7 = (f32[4,2,1,32]{3,0,2,1:T(4,128)S(1)}, f32[4,2,1,32]{3,0,2,1:T(4,128)S(1)}, u32[]{:S(2)}, u32[]{:S(2)}) collective-permute-start(f32[4,2,1,32]{3,0,2,1:T(4,128)S(1)} %get-tuple-element.223), channel_id=1, source_target_pairs={{0,1},{1,2},{2,3},{4,5},{5,6},{6,7},{8,9},{9,10},{10,11},{12,13},{... | collective-permute-start | bytes 3080 | tf_op jit(solution)/shard_map/ppermute | solution.py:30
  293.4 4.9 %collective-permute-start.9 = (f32[3,2,2,32]{3,0,2,1:T(4,128)S(1)}, f32[3,2,2,32]{3,0,2,1:T(4,128)S(1)}, u32[]{:S(2)}, u32[]{:S(2)}) collective-permute-start(f32[3,2,2,32]{3,0,2,1:T(4,128)S(1)} %slice.219), channel_id=1, source_target_pairs={{0,4},{4,8},{8,12},{12,16},{16,20},{20,24},{24,28},{28,32},{32,36}... | collective-permute-start | bytes 4616 | tf_op jit(solution)/shard_map/ppermute | solution.py:19
  378.6 7.9 %collective-permute-start.12 = (f32[3,2,2,32]{3,0,2,1:T(4,128)S(1)}, f32[3,2,2,32]{3,0,2,1:T(4,128)S(1)}, u32[]{:S(2)}, u32[]{:S(2)}) collective-permute-start(f32[3,2,2,32]{3,0,2,1:T(4,128)S(1)} %bitcast.228), channel_id=1, source_target_pairs={{4,0},{8,4},{12,8},{16,12},{20,16},{24,20},{28,24},{32,28},{36,32}... | collective-permute-start | bytes 4616 | tf_op jit(solution)/shard_map/ppermute | solution.py:19
  381.2 10.0 %collective-permute-start.10 = (f32[4,2,1,32]{3,0,2,1:T(4,128)S(1)}, f32[4,2,1,32]{3,0,2,1:T(4,128)S(1)}, u32[]{:S(2)}, u32[]{:S(2)}) collective-permute-start(f32[4,2,1,32]{3,0,2,1:T(4,128)S(1)} %get-tuple-element.222), channel_id=1, source_target_pairs={{1,0},{2,1},{3,2},{5,4},{6,5},{7,6},{9,8},{10,9},{11,10},{13,12},{... | collective-permute-start | bytes 3080 | tf_op jit(solution)/shard_map/ppermute | solution.py:32
  382.5 8.7 %collective-permute-start.11 = (f32[4,2,1,32]{3,0,2,1:T(4,128)S(1)}, f32[4,2,1,32]{3,0,2,1:T(4,128)S(1)}, u32[]{:S(2)}, u32[]{:S(2)}) collective-permute-start(f32[4,2,1,32]{3,0,2,1:T(4,128)S(1)} %get-tuple-element.221), channel_id=1, source_target_pairs={{0,1},{1,2},{2,3},{4,5},{5,6},{6,7},{8,9},{9,10},{10,11},{12,13},{... | collective-permute-start | bytes 3080 | tf_op jit(solution)/shard_map/ppermute | solution.py:30
  387.0 4.9 %collective-permute-start.13 = (f32[3,2,2,32]{3,0,2,1:T(4,128)S(1)}, f32[3,2,2,32]{3,0,2,1:T(4,128)S(1)}, u32[]{:S(2)}, u32[]{:S(2)}) collective-permute-start(f32[3,2,2,32]{3,0,2,1:T(4,128)S(1)} %slice.226), channel_id=1, source_target_pairs={{0,4},{4,8},{8,12},{12,16},{16,20},{20,24},{24,28},{28,32},{32,36}... | collective-permute-start | bytes 4616 | tf_op jit(solution)/shard_map/ppermute | solution.py:19
where the time goes:
time: 475 us; the launch traced here: 473 us
  blocking collectives  234 us (49%)
  other arithmetic  75.1 us (16%)
  starting transfers between devices  40.4 us (9%)
  local copies, waits for them, and re-layouts  37.9 us (8%)
  matrix products  36.5 us (8%)
  waiting for transfers between devices  22.8 us (5%)
  loops' own time  15.5 us (3%)
  between operations  10.9 us (2%)
    psum x3, blocking collectives, body(): lax.psum((jnp.sum(forces * velocity), jnp.sum(velocity * velocity), jnp.s...  234 us
    ppermute x8, starting transfers between devices, passed_along(): return lax.ppermute(x, axis, pairs)  24.5 us
    ppermute x8, waiting for transfers between devices, passed_along(): return lax.ppermute(x, axis, pairs)  22.8 us
    concatenate x4, other arithmetic, spectra(): return jnp.concatenate([real_part, imag_part], axis=-1).astype(jnp.bfloat16)  18.6 us
    dot_general x4, matrix products, spectra(): jnp.einsum('kn,anbc->abkc', forward_rows, halfway, preferred_element_type...  15.8 us
    another operation x1, loops' own time, body(): flow_field = lax.map(pair_flow, (own_spec, target))  15.4 us
    dot_general x4, matrix products, soft_flow(): jnp.einsum('trk,abkjrc->abtjc', inverse_rows, inverse_half, preferred_ele...  14.1 us
    reshape x4, local copies, waits for them, and re-layouts, soft_flow(): inverse_half.reshape(shape_now[0], shape_now[1], PATCH, shape_now[3], 2,...  12.8 us
  transfers between devices with their start and end apart: 14, of which 4 were waited for; matrix products, arithmetic and copies ran while one was open for 17% of the time, Pallas kernels for 0%

commit v1 on v0

v1 whole, which is shorter than its diff:
```python
import functools
import jax
import jax.numpy as jnp
import numpy as np
import ml_dtypes
from jax import lax
from jax.experimental import pallas as pl
from jax.experimental.pallas import tpu as pltpu
from jax.sharding import PartitionSpec as P

PATCH = 64
HALF = 32
REACH = 3
SHARP = 400.0
SCORE_SCALE = SHARP / float(PATCH**4)
LOG2E = 1.4426950408889634
VM = pl.BlockSpec(memory_space=pltpu.VMEM)
SM = pl.BlockSpec(memory_space=pltpu.SMEM)


def host_tables():
    n = np.arange(PATCH)
    angle = ((n[:, None] * n[None, :]) % PATCH) * (2.0 * np.pi / PATCH)
    rounded = lambda a: np.where(np.abs(a) < 1e-9, 0.0, a).astype(ml_dtypes.bfloat16).astype(np.float64)
    cos, sin = rounded(np.cos(angle)), rounded(np.sin(angle))
    z = np.zeros((PATCH, PATCH))
    forward_cols = np.block([[cos, z, sin, z], [z, cos, z, sin]])
    forward_rows = np.concatenate([cos[:32], cos[32:33], sin[1:32]], axis=0)

    def couple(rr, ri, ir, ii):
        return np.block([[rr, z, ri, z], [z, rr, z, ri], [ir, z, ii, z], [z, ir, z, ii]])

    icols = couple(cos, sin, -sin, cos)
    rr, ri, ir, ii = (np.zeros((PATCH, PATCH)) for _ in range(4))
    rr[0] = cos[0]
    rr[1:32] = 2.0 * cos[1:32]
    ir[1:32] = -2.0 * sin[1:32]
    ir[0] = cos[32]
    ri[32] = cos[32]
    ri[33:] = 2.0 * cos[33:]
    ii[33:] = -2.0 * sin[33:]
    ii[32] = cos[0]
    ipack = couple(rr, ri, ir, ii)
    rows = np.zeros((64, 64))
    rows[:, 0] = 1.0
    rows[:, 1:32] = 2.0 * cos[:, 1:32]
    rows[:, 32] = cos[:, 32]
    rows[:, 33:] = -2.0 * sin[:, 1:32]
    spread = np.zeros((2, 64, 128))
    for half in range(2):
        for a in range(2):
            for j in range(2):
                for c in range(16):
                    spread[half, a * 32 + j * 16 + c, j * 64 + a * 32 + 2 * c + half] = 1.0
    bf = lambda a: a.astype(ml_dtypes.bfloat16)
    return dict(fcols=bf(forward_cols), frows=bf(forward_rows), icols=bf(icols), ipack=bf(ipack), irows=bf(rows),
                spread=spread.reshape(128, 128).astype(np.float32))


def half_sums(v, left):
    a = jnp.sum(jnp.where(left, v, 0.0), axis=1, keepdims=True)
    b = jnp.sum(jnp.where(left, 0.0, v), axis=1, keepdims=True)
    return jnp.where(left, a, b)


def tile_stats(x_ref, s, a, mean_ref, rs_ref, width, chunk=512):
    rows = pl.ds(pl.multiple_of(a * PATCH, PATCH), PATCH)
    left = lax.broadcasted_iota(jnp.int32, (1, 128), 1) < 64
    t = s * 2 + a
    scale = 1.0 / PATCH**2
    for c in range(0, width, chunk):
        x = x_ref[s, rows, c:c + chunk].astype(jnp.float32)
        total = jnp.sum(x, axis=0, keepdims=True)
        mean = jnp.concatenate([half_sums(total[:, k:k + 128], left) for k in range(0, chunk, 128)], axis=1) * scale
        mean_ref[t, :, c:c + chunk] = mean
        d = x - mean
        total = jnp.sum(d * d, axis=0, keepdims=True)
        spread = jnp.concatenate([half_sums(total[:, k:k + 128], left) for k in range(0, chunk, 128)], axis=1) * scale
        rs_ref[t, :, c:c + chunk] = lax.rsqrt(spread + 1e-5)


def forward_cols_step(x_ref, s, a, g, groups, mean_ref, rs_ref, fcols, half_ref):
    rows = pl.ds(pl.multiple_of(a * PATCH, PATCH), PATCH)
    t = s * 2 + a
    for i in range(groups):
        cols = pl.ds(pl.multiple_of((g + i) * 128, 128), 128)
        x = x_ref[s, rows, cols].astype(jnp.float32)
        normed = ((x - mean_ref[t, :, cols]) * rs_ref[t, :, cols]).astype(jnp.bfloat16)
        half_ref[:, i * 256:(i + 1) * 256] = jnp.dot(normed, fcols, preferred_element_type=jnp.float32).astype(jnp.bfloat16)


def forward_rows_step(s, a, g, groups, frows, half_ref, spec_ref):
    lane = lax.broadcasted_iota(jnp.int32, (8, 128), 1) % 64
    row0 = lax.broadcasted_iota(jnp.int32, (8, 128), 0) == 0
    upper = lane >= 32
    for i in range(groups):
        both = jnp.dot(frows, half_ref[:, i * 256:(i + 1) * 256], preferred_element_type=jnp.float32)
        ca, cb = both[:HALF, :128], both[:HALF, 128:]
        sa, sb = both[HALF:, :128], both[HALF:, 128:]
        real, imag = ca - sb, sa + cb
        ca, cb, sa, sb = ca[:8], cb[:8], sa[:8], sb[:8]
        real0 = jnp.where(upper, sa, ca)
        imag0 = jnp.where(upper, sb, cb)
        imag0 = jnp.where(lane == 0, pltpu.roll(ca, 96, axis=1), jnp.where(lane == 32, pltpu.roll(sa, 32, axis=1), imag0))
        real = jnp.concatenate([jnp.where(row0, real0, real[:8]), real[8:]], axis=0)
        imag = jnp.concatenate([jnp.where(row0, imag0, imag[:8]), imag[8:]], axis=0)
        spec_ref[s, a, g + i] = jnp.concatenate([real, imag], axis=1).astype(jnp.bfloat16)


def forward_all(x_ref, tiles, mean_ref, rs_ref, fcols_ref, frows_ref, half_ref, spec_ref, width):
    groups = width // 128
    count = x_ref.shape[0] * 2

    def stats(i):
        s, a = tiles(i)
        tile_stats(x_ref, s, a, mean_ref, rs_ref, width)

    def columns(i):
        s, a = tiles(i)
        forward_cols_step(x_ref, s, a, 0, groups, mean_ref, rs_ref, fcols_ref[...], half_ref)

    def rows(i):
        s, a = tiles(i)
        forward_rows_step(s, a, 0, groups, frows_ref[...], half_ref, spec_ref)

    stats(0)
    stats(1)
    columns(0)

    def step(i, _):
        rows(i - 2)
        columns(i - 1)
        stats(i)
        return 0

    lax.fori_loop(2, count, step, 0)
    rows(count - 2)
    columns(count - 1)
    rows(count - 1)


def pair_cross(spec_ref, s, a, c, count, partner, icols, ipack, u_ref):
    lane = lax.broadcasted_iota(jnp.int32, (8, 128), 1) % 32
    row = lax.broadcasted_iota(jnp.int32, (8, 128), 0)
    special = (row == 0) & (lane == 0)
    blocks = []
    for i in range(count):
        mine = spec_ref[s, a, c + i].astype(jnp.float32)
        r, m = mine[:, :128], mine[:, 128:]
        for j in range(2):
            other = spec_ref[partner[j], a, c + i].astype(jnp.float32)
            p, q = other[:, :128], other[:, 128:]
            rp, mq = r * p, m * q
            real, imag = rp + mq, m * p - r * q
            real = jnp.concatenate([jnp.where(special, rp[:8], real[:8]), real[8:]], axis=0)
            imag = jnp.concatenate([jnp.where(special, mq[:8], imag[:8]), imag[8:]], axis=0)
            blocks.append(jnp.concatenate([real, imag], axis=1).astype(jnp.bfloat16))
    n = len(blocks)
    inner = jnp.dot(jnp.concatenate(blocks, axis=0), icols, preferred_element_type=jnp.float32)
    first = jnp.dot(jnp.concatenate([b[:16] for b in blocks], axis=0), ipack, preferred_element_type=jnp.float32)
    row0 = lax.broadcasted_iota(jnp.int32, (8, 256), 0) == 0
    for i in range(n):
        head = jnp.where(row0, first[i * 16:i * 16 + 8], inner[i * 32:i * 32 + 8])
        u = jnp.concatenate([head, inner[i * 32 + 8:i * 32 + 32]], axis=0).astype(jnp.bfloat16)
        u_ref[:32, i * 128:(i + 1) * 128] = u[:, :128]
        u_ref[32:, i * 128:(i + 1) * 128] = u[:, 128:]


def pair_soft(u_ref, n, irows, m_ref, z_ref, r_ref, base):
    for h in range(0, n, 2):
        corr = jnp.dot(irows, u_ref[:, h * 128:(h + 2) * 128], preferred_element_type=jnp.float32)
        for i in (h, h + 1):
            e = [corr[8 * r:8 * r + 8, (i - h) * 128:(i - h + 1) * 128] for r in range(8)]
            m = functools.reduce(jnp.maximum, e)
            e = [jnp.exp2((v - m) * (SCORE_SCALE * LOG2E)) for v in e]
            s3 = e[3]
            s2 = e[2] + s3
            s1 = e[1] + s2
            t4 = e[4]
            t5 = t4 + e[5]
            t6 = t5 + e[6]
            t7 = t6 + e[7]
            spot = pl.ds(pl.multiple_of((base + (i % 2) * 16 + i // 2) * 8, 8), 8)
            m_ref[spot] = m
            z_ref[spot] = (s1 + e[0]) + t7
            r_ref[spot] = ((s1 + s2) + s3) - ((t4 + t5) + (t6 + t7))


def pair_finish(m_ref, z_ref, r_ref, spread_ref):
    rows = m_ref.shape[0] // 8
    lane = lax.broadcasted_iota(jnp.int32, (rows, 128), 1)
    left = lane < 64
    t2 = lane % 64
    shift = jnp.where(t2 < 32, t2, t2 - 64).astype(jnp.float32)
    pick = lambda ref, r: ref[pl.ds(r, rows, stride=8), :]
    top = functools.reduce(jnp.maximum, [pick(m_ref, r) for r in range(8)])
    a = jnp.max(jnp.where(left, top, -jnp.inf), axis=1, keepdims=True)
    b = jnp.max(jnp.where(left, -jnp.inf, top), axis=1, keepdims=True)
    peak = jnp.where(left, a, b)
    total = jnp.zeros((rows, 128), jnp.float32)
    along = jnp.zeros((rows, 128), jnp.float32)
    for r in range(8):
        w = jnp.exp2((pick(m_ref, r) - peak) * (SCORE_SCALE * LOG2E))
        z = pick(z_ref, r)
        total += w * z
        along += w * (8.0 * pick(r_ref, r) + float(r) * z)
    sel = (lax.broadcasted_iota(jnp.int32, (8, 128), 1) // 64 == lax.broadcasted_iota(jnp.int32, (8, 128), 0)).astype(jnp.float32)
    exact = dict(precision=lax.Precision.HIGHEST, preferred_element_type=jnp.float32)
    nt = lambda v: lax.dot_general(sel, v, (((1,), (1,)), ((), ())), **exact)
    tot = nt(total)
    f = [nt(along) / tot, nt(total * shift) / tot]
    both = jnp.concatenate([jnp.concatenate([v[0:1], v[1:2]], axis=1) for v in f] + [jnp.zeros((6, 128), jnp.float32)], axis=0)
    return jnp.dot(both, spread_ref[...], **exact)


def pair_section(spec_ref, s, partner, icols_ref, ipack_ref, irows_ref, spread_ref, u_ref, m_ref, z_ref, r_ref, count=16):
    per = 16 // count
    n = 2 * count

    def cross(i):
        pair_cross(spec_ref, s, i // per, (i % per) * count, count, partner, icols_ref[...], ipack_ref[...], u_ref)

    def soft(i):
        pair_soft(u_ref, n, irows_ref[...], m_ref, z_ref, r_ref, (i // per) * 32 + (i % per) * count)

    cross(0)

    def step(i, _):
        soft(i - 1)
        cross(i)
        return 0

    lax.fori_loop(1, 2 * per, step, 0)
    soft(2 * per - 1)
    return pair_finish(m_ref, z_ref, r_ref, spread_ref)


def emit_flow(s, flow, skip_ref, live_ref, valid_ref, start_ref, flow_ref, pay_ref):
    skip = [skip_ref[s, 0], skip_ref[s, 1]]
    live = [live_ref[s, 0] > 0, live_ref[s, 1] > 0]
    here = [jnp.where(live[j], jnp.concatenate([flow[c:c + 1, j * 64:(j + 1) * 64] for c in range(2)], axis=1), 0.0) for j in range(2)]
    for c in range(2):
        for a in range(2):
            spot = c * 64 + a * 32
            for j in range(2):
                flow_ref[s, j, c, a:a + 1, :] = here[j][:, spot:spot + 32]
    good = jnp.concatenate([valid_ref[s, a:a + 1, :] for _ in range(2) for a in range(2)], axis=1).astype(jnp.float32)
    start = jnp.concatenate([start_ref[s, c, a:a + 1, :] for c in range(2) for a in range(2)], axis=1)
    pay_ref[0, s:s + 1, :] = start
    pay_ref[1, s:s + 1, :] = good
    for d in (1, 2, 3):
        hit = [(skip[j] == d) & live[j] for j in range(2)]
        pay_ref[1 + d, s:s + 1, :] = jnp.where(hit[0] | hit[1], good, 0.0)
        pay_ref[4 + d, s:s + 1, :] = jnp.where(hit[0], here[0], jnp.where(hit[1], here[1], 0.0))


def forward_kernel(x_ref, fcols_ref, frows_ref, spec_ref, mean_ref, rs_ref, half_ref):
    forward_all(x_ref, lambda i: (i // 2, i % 2), mean_ref, rs_ref, fcols_ref, frows_ref, half_ref, spec_ref, x_ref.shape[2])


def forward_call(x, tb):
    s, _, width = x.shape
    return pl.pallas_call(
        forward_kernel,
        out_shape=jax.ShapeDtypeStruct((s, 2, width // 128, HALF, 256), jnp.bfloat16),
        in_specs=[VM] * 3, out_specs=VM,
        scratch_shapes=[pltpu.VMEM((2 * s, 1, width), jnp.float32)] * 2 + [pltpu.VMEM((64, 4096), jnp.bfloat16)],
        compiler_params=pltpu.CompilerParams(vmem_limit_bytes=48 * 2**20),
        name="forward",
    )(x, tb["fcols"], tb["frows"])


def pair_kernel(target_ref, skip_ref, live_ref, valid_ref, start_ref, spec_ref, icols_ref, ipack_ref, irows_ref, spread_ref,
                flow_ref, pay_ref, u_ref, m_ref, z_ref, r_ref):
    for s in range(flow_ref.shape[0]):
        flow = pair_section(spec_ref, s, (target_ref[s, 0], target_ref[s, 1]), icols_ref, ipack_ref, irows_ref, spread_ref,
                            u_ref, m_ref, z_ref, r_ref)
        emit_flow(s, flow, skip_ref, live_ref, valid_ref, start_ref, flow_ref, pay_ref)


def pair_call(target, skips, live, valid, start, spec, tb):
    sections = target.shape[0]
    return pl.pallas_call(
        pair_kernel,
        out_shape=(jax.ShapeDtypeStruct((sections, 2, 2, 2, 32), jnp.float32),
                   jax.ShapeDtypeStruct((8, sections, 128), jnp.float32)),
        in_specs=[SM] * 3 + [VM] * 7, out_specs=(VM, VM),
        scratch_shapes=[pltpu.VMEM((64, 4096), jnp.bfloat16)] + [pltpu.VMEM((512, 128), jnp.float32)] * 3,
        compiler_params=pltpu.CompilerParams(vmem_limit_bytes=48 * 2**20),
        name="pairs",
    )(target, skips, live, valid, start, spec, tb["icols"], tb["ipack"], tb["irows"], tb["spread"])


TINY = 1e-06
STIFF = 0.25
ITERS = 3
FIELDS = 8
BEFORE, AFTER = 3, 3
MESH = pl.DeviceIdType.MESH


def shifted(x, by):
    n = x.shape[0]
    return pltpu.roll(x, (-by) % n, axis=0)


def relax_kernel(nz, nx, step_ref, mix_ref, pay_ref, out_ref, ext, part1, part2, sem_a, got_a, sem_1, got_1, sem_2, got_2):
    gz = lax.axis_index("gz")
    xy = lax.axis_index("xy")
    groups = nz // 4
    yy, zc = gz // groups, gz % groups
    halo = [(db, dx) for db in range(-BEFORE, AFTER + 1) for dx in (-1, 0, 1) if (db, dx) != (0, 0)]

    def at(db, dx):
        return (lax.rem(gz + db + nz, nz), lax.rem(xy + dx + nx, nx))

    def near(r):
        k = lax.rem(yy * nx + xy + r, 4 * nx)
        return (k // nx * groups + zc, lax.rem(k, nx))

    def along(r):
        return (yy * groups + lax.rem(zc + r, groups), xy)

    barrier = pltpu.get_barrier_semaphore()
    for db, dx in halo:
        pl.semaphore_signal(barrier, inc=1, device_id=at(db, dx), device_id_type=MESH)
    for r in range(1, 4 * nx):
        pl.semaphore_signal(barrier, inc=1, device_id=near(r), device_id_type=MESH)
    for r in range(1, groups):
        pl.semaphore_signal(barrier, inc=1, device_id=along(r), device_id_type=MESH)
    pl.semaphore_wait(barrier, len(halo) + 4 * nx - 1 + groups - 1)

    copies = []
    for n, (db, dx) in enumerate(halo):
        copies.append(pltpu.make_async_remote_copy(
            src_ref=pay_ref, dst_ref=ext.at[dx + 1, db + BEFORE], send_sem=sem_a.at[n], recv_sem=got_a.at[n],
            device_id=at(-db, -dx), device_id_type=MESH))
        copies[-1].start()
    ext[1, BEFORE] = pay_ref[...]
    for c in copies:
        c.wait()

    blocks = BEFORE + AFTER + 1
    own = slice(4 * BEFORE, 4 * BEFORE + 4)
    lane = lax.broadcasted_iota(jnp.int32, (4 * blocks + 4, 128), 1)
    col = lane % 32
    upper = (lane // 32) % 2 == 0
    inside = [jnp.where(xy > 0, 1.0, 0.0), 1.0, jnp.where(xy < nx - 1, 1.0, 0.0)]

    def field(dx, f):
        return jnp.concatenate([ext[dx, k, f] for k in range(blocks)] + [jnp.zeros((4, 128), jnp.float32)], axis=0)

    vel, bias, weights = [], [], []
    for dx in range(3):
        valid = field(dx, 1)
        total = jnp.zeros_like(valid)
        ws = []
        for d in (1, 2, 3):
            w = field(dx, 1 + d) * shifted(valid, d)
            wf = w * field(dx, 4 + d)
            total += shifted(wf, -d) - wf
            ws.append(w)
        weights.append(ws)
        bias.append(total * inside[dx])
        vel.append(field(dx, 0) * inside[dx])

    def force(fields, dx):
        v = fields[dx]
        above = fields[dx - 1] if dx > 0 else jnp.zeros_like(v)
        below = fields[dx + 1] if dx < 2 else jnp.zeros_like(v)
        lateral = jnp.where(col == 0, 0.0, pltpu.roll(v, 1, axis=1)) + jnp.where(col == 31, 0.0, pltpu.roll(v, 127, axis=1))
        down, up = pltpu.roll(v, 32, axis=1), pltpu.roll(v, 96, axis=1)
        vertical = jnp.where(upper, pltpu.roll(above, 96, axis=1) + up, down + pltpu.roll(below, 32, axis=1))
        out = STIFF * (lateral + vertical - 4.0 * v)
        for d in (1, 2, 3):
            pull = weights[dx][d - 1] * (shifted(v, d) - v)
            out += pull - shifted(pull, -d)
        return out * inside[dx]

    av = [force(vel, dx) for dx in range(3)]
    ab = [force(bias, dx) for dx in range(3)]
    aav, aab = force(av, 1), force(ab, 1)
    basis = [x[own] for x in (vel[1], bias[1], av[1], ab[1], aav, aab)]

    index = {}
    rows = []
    for i in range(6):
        for j in range(i, 6):
            index[i, j] = index[j, i] = len(rows)
            rows.append(jnp.sum(basis[i] * basis[j], axis=0, keepdims=True))
    rows += [jnp.zeros_like(rows[0])] * 3
    part1[0] = jnp.concatenate(rows, axis=0)

    def reduce(part, count, peer, sem, got):
        sends = []
        for r in range(1, count):
            sends.append(pltpu.make_async_remote_copy(
                src_ref=part.at[0], dst_ref=part.at[r], send_sem=sem.at[r], recv_sem=got.at[r],
                device_id=peer(r), device_id_type=MESH))
            sends[-1].start()
        for c in sends:
            c.wait()
        return functools.reduce(jnp.add, [part[r] for r in range(count)])

    part2[0] = reduce(part1, 4 * nx, near, sem_1, got_1)
    gram = jnp.sum(reduce(part2, groups, along, sem_2, got_2), axis=1, keepdims=True)
    gram = jnp.broadcast_to(gram, (24, 128))
    g = {k: gram[n:n + 1] for k, n in index.items()}

    def dot(p, q):
        terms = [p[i] * q[j] * g[i, j] for i in range(6) for j in range(6) if p[i] is not None and q[j] is not None]
        return functools.reduce(jnp.add, terms)

    def plus(*xs):
        xs = [x for x in xs if x is not None]
        return functools.reduce(jnp.add, xs) if xs else None

    def times(k, x):
        return None if x is None else k * x

    one = jnp.ones((1, 128), jnp.float32)
    v = [one] + [None] * 5
    d = [None] * 6
    for it in range(ITERS):
        f = [None, one] + d[:4]
        power, speed, strength = dot(f, v), dot(v, v), dot(f, f)
        speed, strength = jnp.maximum(speed, 0.0), jnp.maximum(strength, 0.0)
        gating = 0.5 + 0.5 * power / jnp.sqrt((speed + TINY) * (strength + TINY))
        ratio = jnp.sqrt((speed + TINY) / (strength + TINY))
        mix, step = mix_ref[it], step_ref[it]
        kv, kf = gating * (1.0 - mix), gating * (mix * ratio) + step
        v = [plus(times(kv, v[i]), times(kf, f[i])) for i in range(6)]
        d = [plus(d[i], times(step, v[i])) for i in range(6)]
    result = functools.reduce(jnp.add, [d[i] * basis[i] for i in range(6)])
    for c in range(2):
        for a in range(2):
            at0 = c * 64 + a * 32
            for s in range(4):
                out_ref[s, c, a:a + 1, :] = result[s:s + 1, at0:at0 + 32]


def relax_call(step, mix, payload, nz, nx):
    vm = pl.BlockSpec(memory_space=pltpu.VMEM)
    sm = pl.BlockSpec(memory_space=pltpu.SMEM)
    dma = pltpu.SemaphoreType.DMA
    blocks = BEFORE + AFTER + 1
    return pl.pallas_call(
        functools.partial(relax_kernel, nz, nx),
        out_shape=jax.ShapeDtypeStruct((4, 2, 2, 32), jnp.float32),
        in_specs=[sm, sm, vm], out_specs=vm,
        scratch_shapes=[
            pltpu.VMEM((3, blocks, FIELDS, 4, 128), jnp.float32),
            pltpu.VMEM((4 * nx, 24, 128), jnp.float32),
            pltpu.VMEM((nz // 4, 24, 128), jnp.float32),
            dma((3 * blocks,)), dma((3 * blocks,)), dma((4 * nx,)), dma((4 * nx,)), dma((nz // 4,)), dma((nz // 4,)),
        ],
        compiler_params=pltpu.CompilerParams(collective_id=0, has_side_effects=True, vmem_limit_bytes=32 * 2**20),
        name="relax",
    )(step, mix, payload)


def body(sections, skips, patch_valid, velocity_start, step_size, mixing):
    tb = {k: jnp.asarray(v) for k, v in host_tables().items()}
    count = sections.shape[0]
    nz, nx = lax.axis_size("gz"), lax.axis_size("xy")
    first = lax.axis_index("gz") * count
    target = jnp.arange(count, dtype=jnp.int32)[:, None] + skips
    live = ((skips > 0) & (first + target < count * nz)).astype(jnp.int32)
    own = forward_call(sections, tb)
    far = lax.ppermute(own[:REACH], "gz", [(i, (i - 1) % nz) for i in range(nz)])
    spec = jnp.concatenate([own, far], axis=0)
    flow, payload = pair_call(target, skips, live, patch_valid, velocity_start, spec, tb)
    displace = relax_call(step_size, mixing, payload, nz, nx)
    return flow, displace


def solution(mesh):
    in_specs = (
        P("gz", "xy", None),
        P("gz", None),
        P("gz", "xy", None),
        P("gz", None, "xy", None),
        P(),
        P(),
    )
    out_specs = (P("gz", None, None, "xy", None), P("gz", None, "xy", None))
    return jax.shard_map(body, mesh=mesh, in_specs=in_specs, out_specs=out_specs, check_vma=False)
```

time: 475 us -> 74.4 us (0.16)
  blocking collectives: 234 us -> 0 us
  other arithmetic: 75.1 us -> 1.74 us
  Pallas kernels: 0 us -> 45.2 us
  starting transfers between devices: 40.4 us -> 3.24 us
  matrix products: 36.5 us -> 0 us
  local copies, waits for them, and re-layouts: 37.9 us -> 5.17 us
  loops' own time: 15.5 us -> 0 us
  between operations: 10.9 us -> 0.77 us
  waiting for transfers between devices: 22.8 us -> 18 us
    psum x3 -> x0, blocking collectives: 234 us -> none  [body(): lax.psum((jnp.sum(forces * velocity), jnp.sum(velocity * velocity), jnp.s...]
    pallas_call x0 -> x3, Pallas kernels: none -> 45.2 us  [the longest x1 32.4 us: relax_call(): pl.pallas_call(functools.partial(relax_kernel, nz, nx), out_shape=jax.Sha...]
    ppermute x14 -> x1, starting transfers between devices: 40.4 us -> 3.24 us  [body(): lax.ppermute(own[:REACH], 'gz', [(i, (i - 1) % nz) for i in range(nz)])]
    dot_general x18 -> x0, matrix products: 36.5 us -> none  [the longest x4 15.8 us: spectra(): jnp.einsum('kn,anbc->abkc', forward_rows, halfway, preferred_element_type...]
    concatenate x10 -> x1, other arithmetic: 24.7 us -> 1.72 us  [body(): spec = jnp.concatenate([own, far], axis=0)]
    reduce_sum x16 -> x0, other arithmetic: 21.5 us -> none  [the longest x4 9.58 us: soft_flow(): jnp.sum(soft_weights * shifts[None, None, :, None, None], axis=(2, 4))]
    another operation x2 -> x0, loops' own time: 15.5 us -> none  [the longest x1 15.4 us: body(): flow_field = lax.map(pair_flow, (own_spec, target))]
    reshape x4 -> x0, local copies, waits for them, and re-layouts: 12.8 us -> none  [soft_flow(): inverse_half.reshape(shape_now[0], shape_now[1], PATCH, shape_now[3], 2,...]
  transfers between devices with their start and end apart: 14 -> 1, of which waited for: 4 -> 1; matrix products, arithmetic and copies ran while one was open for 17% -> 0% of each run, Pallas kernels for 0% -> 0%
where the time goes in v1:
time: 74.4 us; the launch traced here: 74.1 us
  Pallas kernels  45.2 us (61%)
  waiting for transfers between devices  18 us (24%)
  local copies, waits for them, and re-layouts  5.17 us (7%)
  starting transfers between devices  3.24 us (4%)
  other arithmetic  1.74 us (2%)
  between operations  0.77 us (1%)
    pallas_call x1, Pallas kernels, relax_call(): pl.pallas_call(functools.partial(relax_kernel, nz, nx), out_shape=jax.Sha...  32.4 us
    ppermute x1, waiting for transfers between devices, body(): lax.ppermute(own[:REACH], 'gz', [(i, (i - 1) % nz) for i in range(nz)])  18 us
    pallas_call x1, Pallas kernels, pair_call(): pl.pallas_call(pair_kernel, out_shape=(jax.ShapeDtypeStruct((sections, 2,...  8.51 us
    pallas_call x1, Pallas kernels, forward_call(): pl.pallas_call(forward_kernel, out_shape=jax.ShapeDtypeStruct((s, 2, widt...  4.26 us
    unnamed x26, local copies, waits for them, and re-layouts  3.89 us
    ppermute x1, starting transfers between devices, body(): lax.ppermute(own[:REACH], 'gz', [(i, (i - 1) % nz) for i in range(nz)])  3.24 us
    concatenate x1, other arithmetic, body(): spec = jnp.concatenate([own, far], axis=0)  1.72 us
  transfers between devices with their start and end apart: 1, of which 1 were waited for; matrix products, arithmetic and copies ran while one was open for 0% of the time, Pallas kernels for 0%

profile of v1, /device:TPU:1, one launch (start us, length us, event | category | flops | bytes accessed | tf_op | source)
XLA Modules:
  0.0 74.1 jit_solution(12388161273493448935)
XLA Ops:
  0.6 0.0 copy-start
  0.6 1.6 %copy-done = bf16[4,128,2048]{2,1,0:T(8,128)(2,1)S(1)} copy-done((bf16[4,128,2048]{2,1,0:T(8,128)(2,1)S(1)}, bf16[4,128,2048]{2,1,0:T(8,128)(2,1)}, u32[]{:S(2)}) %copy-start) | copy-done | bytes 2097176
  2.2 0.0 copy-start.4
  2.2 0.8 %copy-done.4 = bf16[128,256]{1,0:T(8,128)(2,1)S(1)} copy-done((bf16[128,256]{1,0:T(8,128)(2,1)S(1)}, bf16[128,256]{1,0:T(8,128)(2,1)}, u32[]{:S(2)}) %copy-start.4) | copy-done | bytes 65560
  3.1 0.0 copy-start.6
  3.1 0.7 copy-done.6
  3.8 4.3 %forward.1 = bf16[4,2,16,32,256]{4,3,2,1,0:T(8,128)(2,1)S(1)} custom-call(bf16[4,128,2048]{2,1,0:T(8,128)(2,1)S(1)} %copy-done, bf16[128,256]{1,0:T(8,128)(2,1)S(1)} %copy-done.4, bf16[64,64]{1,0:T(8,128)(2,1)S(1)} %copy-done.6), custom_call_target="tpu_custom_call" | custom-call | tf_op jit(solution)/shard_map/forward/pallas_call | solution.py:263
  8.0 0.0 copy-start.11
  8.0 1.3 %slice.4 = bf16[3,2,16,32,256]{4,3,2,1,0:T(8,128)(2,1)} slice(bf16[4,2,16,32,256]{4,3,2,1,0:T(8,128)(2,1)S(1)} %forward.1), slice={[0:3], [0:2], [0:16], [0:32], [0:256]} | slice | bytes 3145728 | tf_op jit(solution)/shard_map/slice | solution.py:470
  9.3 3.2 %collective-permute-start = (bf16[3,2,16,32,256]{4,3,2,1,0:T(8,128)(2,1)}, bf16[3,2,16,32,256]{4,3,2,1,0:T(8,128)(2,1)}, u32[]{:S(2)}, u32[]{:S(2)}) collective-permute-start(bf16[3,2,16,32,256]{4,3,2,1,0:T(8,128)(2,1)} %slice.4), channel_id=1, source_target_pairs={{0,252},{4,0},{8,4},{12,8},{16,12},{20,16},{24,20},{28,24},{32,28}... | collective-permute-start | bytes 4718600 | tf_op jit(solution)/shard_map/ppermute | solution.py:470
  12.6 0.0 copy-done.11
  12.6 0.1 copy.14.skip_ref
  12.7 0.0 copy-start.1
  12.7 0.0 copy-start.2
  12.7 0.0 copy-start.3
  12.7 0.0 copy-start.5
  12.7 0.0 copy-start.7
  12.7 0.0 copy-start.8
  12.8 18.0 %collective-permute-done = bf16[3,2,16,32,256]{4,3,2,1,0:T(8,128)(2,1)} collective-permute-done((bf16[3,2,16,32,256]{4,3,2,1,0:T(8,128)(2,1)}, bf16[3,2,16,32,256]{4,3,2,1,0:T(8,128)(2,1)}, u32[]{:S(2)}, u32[]{:S(2)}) %collective-permute-start) | collective-permute-done | bytes 1572896 | tf_op jit(solution)/shard_map/ppermute | solution.py:470
  30.8 1.7 %pad_maximum_fusion.spec_ref = bf16[7,2,16,32,256]{4,3,2,1,0:T(8,128)(2,1)S(1)} fusion(bf16[3,2,16,32,256]{4,3,2,1,0:T(8,128)(2,1)} %collective-permute-done, bf16[4,2,16,32,256]{4,3,2,1,0:T(8,128)(2,1)S(1)} %forward.1), kind=kLoop, calls=%fused_computation | loop fusion | flops 1835008 | bytes 7340032 | tf_op jit(solution)/shard_map/concatenate | solution.py:471
  32.5 0.0 copy-done.1
  32.5 0.0 copy-done.2
  32.5 0.0 copy-done.3
  32.5 0.0 copy-done.5
  32.5 0.0 copy-done.7
  32.6 0.0 copy-done.8
  32.6 0.0 copy-start.9
  32.6 0.0 copy-start.10
  32.6 8.5 %pairs.1 = (f32[4,2,2,2,32]{4,3,2,1,0:T(2,128)}, f32[8,4,128]{2,1,0:T(4,128)S(1)}) custom-call(s32[4,2]{1,0:T(4,128)S(1)} %iota_add_fusion.target_ref, s32[4,2]{1,0:T(4,128)S(1)} %copy.14.skip_ref, s32[4,2]{1,0:T(4,128)S(1)} %fusion.1.live_ref, s32[4,2,32]{2,1,0:T(2,128)S(1)} %copy-done.8, f32[4,2,2,32]{3,2,1,0:T(2,128)S(1)} %copy-done.7, ...), custom_call_target="tpu_custom_call" | custom-call | tf_op jit(solution)/shard_map/pairs/pallas_call | solution.py:283
  41.1 0.0 copy-done.9
  41.1 0.0 copy-done.10
  41.1 32.4 %relax.1 = f32[4,2,2,32]{3,2,1,0:T(2,128)S(1)} custom-call(f32[3]{0:T(128)S(1)} %copy-done.9, f32[3]{0:T(128)S(1)} %copy-done.10, f32[8,4,128]{2,1,0:T(4,128)S(1)} %get-tuple-element.5.pay_ref), custom_call_target="tpu_custom_call" | custom-call | tf_op jit(solution)/shard_map/relax/pallas_call | solution.py:447
  73.5 0.6 copy.18
  (2 shorter events, 0.0 us)
Async XLA Ops:
  0.6 1.6 %copy-start = (bf16[4,128,2048]{2,1,0:T(8,128)(2,1)S(1)}, bf16[4,128,2048]{2,1,0:T(8,128)(2,1)}, u32[]{:S(2)}) copy-start(bf16[4,128,2048]{2,1,0:T(8,128)(2,1)} %x_ref.1) | copy-start | bytes 6291460
  2.2 0.8 %copy-start.4 = (bf16[128,256]{1,0:T(8,128)(2,1)S(1)}, bf16[128,256]{1,0:T(8,128)(2,1)}, u32[]{:S(2)}) copy-start(bf16[128,256]{1,0:T(8,128)(2,1)} %constant.24.clone.fcols_ref) | copy-start | bytes 196612
  3.1 0.7 copy-start.6
  8.0 4.5 %copy-start.11 = (s32[4,2]{0,1:T(2,128)S(1)}, s32[4,2]{0,1:T(2,128)}, u32[]{:S(2)}) copy-start(s32[4,2]{0,1:T(2,128)} %param.13) | copy-start | bytes 100
  9.3 21.4 %collective-permute-start = (bf16[3,2,16,32,256]{4,3,2,1,0:T(8,128)(2,1)}, bf16[3,2,16,32,256]{4,3,2,1,0:T(8,128)(2,1)}, u32[]{:S(2)}, u32[]{:S(2)}) collective-permute-start(bf16[3,2,16,32,256]{4,3,2,1,0:T(8,128)(2,1)} %slice.4), channel_id=1, source_target_pairs={{0,252},{4,0},{8,4},{12,8},{16,12},{20,16},{24,20},{28,24},{32,28}... | collective-permute-start | bytes 4718600 | tf_op jit(solution)/shard_map/ppermute | solution.py:470
  12.7 19.8 %copy-start.1 = (bf16[256,256]{1,0:T(8,128)(2,1)S(1)}, bf16[256,256]{1,0:T(8,128)(2,1)}, u32[]{:S(2)}) copy-start(bf16[256,256]{1,0:T(8,128)(2,1)} %constant.26.clone.icols_ref) | copy-start | bytes 393220
  12.7 19.8 %copy-start.2 = (bf16[256,256]{1,0:T(8,128)(2,1)S(1)}, bf16[256,256]{1,0:T(8,128)(2,1)}, u32[]{:S(2)}) copy-start(bf16[256,256]{1,0:T(8,128)(2,1)} %constant.27.clone.ipack_ref) | copy-start | bytes 393220
  12.7 19.8 %copy-start.3 = (f32[128,128]{1,0:T(8,128)S(1)}, f32[128,128]{1,0:T(8,128)}, u32[]{:S(2)}) copy-start(f32[128,128]{1,0:T(8,128)} %constant.29.clone.spread_ref) | copy-start | bytes 196612
  12.7 19.8 %copy-start.5 = (bf16[64,64]{1,0:T(8,128)(2,1)S(1)}, bf16[64,64]{1,0:T(8,128)(2,1)}, u32[]{:S(2)}) copy-start(bf16[64,64]{1,0:T(8,128)(2,1)} %constant.28.clone.irows_ref) | copy-start | bytes 24580
  12.7 19.8 %copy-start.7 = (f32[4,2,2,32]{3,2,1,0:T(2,128)S(1)}, f32[4,2,2,32]{3,2,1,0:T(2,128)}, u32[]{:S(2)}) copy-start(f32[4,2,2,32]{3,2,1,0:T(2,128)} %start_ref.1) | copy-start | bytes 6148
  12.7 19.8 %copy-start.8 = (s32[4,2,32]{2,1,0:T(2,128)S(1)}, s32[4,2,32]{2,1,0:T(2,128)}, u32[]{:S(2)}) copy-start(s32[4,2,32]{2,1,0:T(2,128)} %valid_ref.1) | copy-start | bytes 3076
  32.6 8.5 %copy-start.9 = (f32[3]{0:T(128)S(1)}, f32[3]{0:T(128)}, u32[]{:S(2)}) copy-start(f32[3]{0:T(128)} %step_ref.1) | copy-start | bytes 40
  32.6 8.5 %copy-start.10 = (f32[3]{0:T(128)S(1)}, f32[3]{0:T(128)}, u32[]{:S(2)}) copy-start(f32[3]{0:T(128)} %mix_ref.1) | copy-start | bytes 40

commit v2 on v1

v2 whole, which is shorter than its diff:
```python
import functools
import jax
import jax.numpy as jnp
import numpy as np
import ml_dtypes
from jax import lax
from jax.experimental import pallas as pl
from jax.experimental.pallas import tpu as pltpu
from jax.sharding import PartitionSpec as P

PATCH = 64
HALF = 32
ITERS = 3
SHARP = 400.0
STIFF = 0.25
TINY = 1e-06
LOG2E = 1.4426950408889634
SCORE_EXP = SHARP / float(PATCH**4) * LOG2E
MESH = pl.DeviceIdType.MESH
STEPS = 11
NEAR, FAR = 2, 3


def host_tables():
    n = np.arange(PATCH)
    angle = ((n[:, None] * n[None, :]) % PATCH) * (2.0 * np.pi / PATCH)
    rounded = lambda a: np.where(np.abs(a) < 1e-9, 0.0, a).astype(ml_dtypes.bfloat16).astype(np.float64)
    cos, sin = rounded(np.cos(angle)), rounded(np.sin(angle))
    z = np.zeros((PATCH, PATCH))
    forward_cols = np.block([[cos, z, sin, z], [z, cos, z, sin]])
    forward_rows = np.concatenate([cos[:32], cos[32:33], sin[1:32]], axis=0)

    def couple(rr, ri, ir, ii):
        return np.block([[rr, z, ri, z], [z, rr, z, ri], [ir, z, ii, z], [z, ir, z, ii]])

    icols = couple(cos, sin, -sin, cos)
    rr, ri, ir, ii = (np.zeros((PATCH, PATCH)) for _ in range(4))
    rr[0] = cos[0]
    rr[1:32] = 2.0 * cos[1:32]
    ir[1:32] = -2.0 * sin[1:32]
    ir[0] = cos[32]
    ri[32] = cos[32]
    ri[33:] = 2.0 * cos[33:]
    ii[33:] = -2.0 * sin[33:]
    ii[32] = cos[0]
    ipack = couple(rr, ri, ir, ii)
    inverse_rows = np.zeros((64, 64))
    inverse_rows[:, 0] = 1.0
    inverse_rows[:, 1:32] = 2.0 * cos[:, 1:32]
    inverse_rows[:, 32] = cos[:, 32]
    inverse_rows[:, 33:] = -2.0 * sin[:, 1:32]
    last = np.concatenate([forward_rows, z, inverse_rows, z], axis=1)
    return np.concatenate([forward_cols, icols, ipack, last], axis=0).astype(ml_dtypes.bfloat16)


def half_sums(v, left):
    a = jnp.sum(jnp.where(left, v, 0.0), axis=1, keepdims=True)
    b = jnp.sum(jnp.where(left, 0.0, v), axis=1, keepdims=True)
    return jnp.where(left, a, b)


def tile_stats(x_ref, s, a, mean_ref, rs_ref, chunk=512):
    rows = pl.ds(pl.multiple_of(a * PATCH, PATCH), PATCH)
    left = lax.broadcasted_iota(jnp.int32, (1, 128), 1) < 64
    t = s * 2 + a
    scale = 1.0 / PATCH**2
    spans = range(0, chunk, 128)
    for c in range(0, x_ref.shape[2], chunk):
        x = x_ref[s, rows, c:c + chunk].astype(jnp.float32)
        total = jnp.sum(x, axis=0, keepdims=True)
        mean = jnp.concatenate([half_sums(total[:, k:k + 128], left) for k in spans], axis=1) * scale
        mean_ref[t, :, c:c + chunk] = mean
        d = x - mean
        total = jnp.sum(d * d, axis=0, keepdims=True)
        spread = jnp.concatenate([half_sums(total[:, k:k + 128], left) for k in spans], axis=1) * scale
        rs_ref[t, :, c:c + chunk] = lax.rsqrt(spread + 1e-5)


def tile_columns(x_ref, s, a, mean_ref, rs_ref, fcols, half_ref):
    rows = pl.ds(pl.multiple_of(a * PATCH, PATCH), PATCH)
    t = s * 2 + a
    for i in range(x_ref.shape[2] // 128):
        cols = slice(i * 128, (i + 1) * 128)
        x = x_ref[s, rows, cols].astype(jnp.float32)
        normed = ((x - mean_ref[t, :, cols]) * rs_ref[t, :, cols]).astype(jnp.bfloat16)
        half_ref[:, i * 256:(i + 1) * 256] = jnp.dot(normed, fcols, preferred_element_type=jnp.float32).astype(jnp.bfloat16)


def tile_rows(s, a, frows, half_ref, spec_ref):
    lane = lax.broadcasted_iota(jnp.int32, (8, 128), 1) % 64
    row0 = lax.broadcasted_iota(jnp.int32, (8, 128), 0) == 0
    upper = lane >= 32
    for i in range(spec_ref.shape[1]):
        both = jnp.dot(frows, half_ref[:, i * 256:(i + 1) * 256], preferred_element_type=jnp.float32)
        ca, cb = both[:HALF, :128], both[:HALF, 128:]
        sa, sb = both[HALF:, :128], both[HALF:, 128:]
        real, imag = ca - sb, sa + cb
        ca, cb, sa, sb = ca[:8], cb[:8], sa[:8], sb[:8]
        real0 = jnp.where(upper, sa, ca)
        imag0 = jnp.where(upper, sb, cb)
        imag0 = jnp.where(lane == 0, pltpu.roll(ca, 96, axis=1), jnp.where(lane == 32, pltpu.roll(sa, 32, axis=1), imag0))
        real = jnp.concatenate([jnp.where(row0, real0, real[:8]), real[8:]], axis=0)
        imag = jnp.concatenate([jnp.where(row0, imag0, imag[:8]), imag[8:]], axis=0)
        spec_ref[s * 2 + a, i] = jnp.concatenate([real, imag], axis=1).astype(jnp.bfloat16)


def pair_cross(tasks, count, icols, ipack, u_ref):
    lane = lax.broadcasted_iota(jnp.int32, (8, 128), 1) % 32
    row = lax.broadcasted_iota(jnp.int32, (8, 128), 0)
    special = (row == 0) & (lane == 0)
    blocks = []
    for mine_of, other_of in tasks:
        for i in range(count):
            mine, other = mine_of(i).astype(jnp.float32), other_of(i).astype(jnp.float32)
            r, m = mine[:, :128], mine[:, 128:]
            p, q = other[:, :128], other[:, 128:]
            rp, mq = r * p, m * q
            real, imag = rp + mq, m * p - r * q
            real = jnp.concatenate([jnp.where(special, rp[:8], real[:8]), real[8:]], axis=0)
            imag = jnp.concatenate([jnp.where(special, mq[:8], imag[:8]), imag[8:]], axis=0)
            blocks.append(jnp.concatenate([real, imag], axis=1).astype(jnp.bfloat16))
    n = len(blocks)
    inner = jnp.dot(jnp.concatenate(blocks, axis=0), icols, preferred_element_type=jnp.float32)
    first = jnp.dot(jnp.concatenate([b[:16] for b in blocks], axis=0), ipack, preferred_element_type=jnp.float32)
    row0 = lax.broadcasted_iota(jnp.int32, (8, 256), 0) == 0
    for i in range(n):
        head = jnp.where(row0, first[i * 16:i * 16 + 8], inner[i * 32:i * 32 + 8])
        u = jnp.concatenate([head, inner[i * 32 + 8:i * 32 + 32]], axis=0).astype(jnp.bfloat16)
        u_ref[:32, i * 128:(i + 1) * 128] = u[:, :128]
        u_ref[32:, i * 128:(i + 1) * 128] = u[:, 128:]


def pair_soft(u_ref, n, irows, m_ref, z_ref, r_ref, step):
    for h in range(0, n, 2):
        corr = jnp.dot(irows, u_ref[:, h * 128:(h + 2) * 128], preferred_element_type=jnp.float32)
        for i in (h, h + 1):
            e = [corr[8 * r:8 * r + 8, (i - h) * 128:(i - h + 1) * 128] for r in range(8)]
            m = functools.reduce(jnp.maximum, e)
            e = [jnp.exp2((v - m) * SCORE_EXP) for v in e]
            s3 = e[3]
            s2 = e[2] + s3
            s1 = e[1] + s2
            t4 = e[4]
            t5 = t4 + e[5]
            t6 = t5 + e[6]
            t7 = t6 + e[7]
            spot = pl.ds(pl.multiple_of((step * n + i) * 8, 8), 8)
            m_ref[spot] = m
            z_ref[spot] = (s1 + e[0]) + t7
            r_ref[spot] = ((s1 + s2) + s3) - ((t4 + t5) + (t6 + t7))


def pair_finish(m_ref, z_ref, r_ref, first, count):
    rows = count * 32
    lane = lax.broadcasted_iota(jnp.int32, (rows, 128), 1)
    left = lane < 64
    t2 = lane % 64
    shift = jnp.where(t2 < 32, t2, t2 - 64).astype(jnp.float32)
    pick = lambda ref, r: ref[pl.ds(first * 256 + r, rows, stride=8), :]
    top = functools.reduce(jnp.maximum, [pick(m_ref, r) for r in range(8)])
    a = jnp.max(jnp.where(left, top, -jnp.inf), axis=1, keepdims=True)
    b = jnp.max(jnp.where(left, -jnp.inf, top), axis=1, keepdims=True)
    peak = jnp.where(left, a, b)
    total = jnp.zeros((rows, 128), jnp.float32)
    along = jnp.zeros((rows, 128), jnp.float32)
    for r in range(8):
        w = jnp.exp2((pick(m_ref, r) - peak) * SCORE_EXP)
        z = pick(z_ref, r)
        total += w * z
        along += w * (8.0 * pick(r_ref, r) + float(r) * z)
    across = total * shift

    def sides(v):
        return (jnp.sum(jnp.where(left, v, 0.0), axis=1, keepdims=True), jnp.sum(jnp.where(left, 0.0, v), axis=1, keepdims=True))

    owner = lax.broadcasted_iota(jnp.int32, (rows, 128), 0) % 32
    mine = (lane % 64) // 2 == owner
    odd = lane % 2 == 1
    (tl, tr), (al, ar), (cl, cr) = sides(total), sides(along), sides(across)
    down = jnp.where(mine, jnp.where(odd, tr, tl), 0.0)
    up = jnp.where(mine, jnp.where(left, jnp.where(odd, ar, al), jnp.where(odd, cr, cl)), 0.0)
    fold = lambda v: [jnp.sum(v[k * 32:(k + 1) * 32], axis=0, keepdims=True) for k in range(count)]
    return [u / d for u, d in zip(fold(up), fold(down))]


def shifted(x, by):
    return pltpu.roll(x, (-by) % x.shape[0], axis=0)


def kernel(nz, nx, x_hbm, tab_hbm, skip_ref, step_ref, mix_ref, valid_ref, start_ref, flow_ref, out_ref,
           x_ref, tab_ref, mean_ref, rs_ref, half_ref, spec_ref, recv_ref, u_ref, m_ref, z_ref, r_ref,
           ext_ref, push_ref, back_ref, sent_ref, part1, part2,
           sem_x, sem_tab, sem_s, got_s, sem_e, got_e, sem_l, got_l, sem_b, got_b, sem_1, got_1, sem_2, got_2):
    gz = lax.axis_index("gz")
    xy = lax.axis_index("xy")
    groups = nz // 4
    yy, zc = gz // groups, gz % groups
    couples = spec_ref.shape[1]

    loads = [pltpu.make_async_copy(x_hbm.at[s], x_ref.at[s], sem_x.at[s]) for s in range(4)]
    for c in loads:
        c.start()
    tab_load = pltpu.make_async_copy(tab_hbm, tab_ref, sem_tab)
    tab_load.start()

    def at(db, dx):
        return (lax.rem(gz + db + nz, nz), lax.rem(xy + dx + nx, nx))

    def near(r):
        k = lax.rem(yy * nx + xy + r, 4 * nx)
        return (k // nx * groups + zc, lax.rem(k, nx))

    def along(r):
        return (yy * groups + lax.rem(zc + r, groups), xy)

    wide = [(db, dx) for db in range(-FAR, FAR + 1) for dx in (-1, 0, 1) if (db, dx) != (0, 0)]
    close = [(db, dx) for db, dx in wide if abs(db) <= NEAR]
    barrier = pltpu.get_barrier_semaphore()
    peers = [at(db, dx) for db, dx in wide] + [near(r) for r in range(1, 4 * nx)] + [along(r) for r in range(1, groups)]
    for peer in peers:
        pl.semaphore_signal(barrier, inc=1, device_id=peer, device_id_type=MESH)

    lanes = lax.broadcasted_iota(jnp.int32, (1, 128), 1)
    skip = [[skip_ref[s, j] for j in range(2)] for s in range(4)]
    live = [[(k > 0) & (gz * 4 + s + k < 4 * nz) for k in skip[s]] for s in range(4)]
    for s in range(4):
        ext_ref[1, NEAR, 0, s:s + 1, :] = jnp.concatenate(
            [start_ref[s, c, a:a + 1, :] for c in range(2) for a in range(2)], axis=1)
        row = jnp.concatenate([valid_ref[s, a:a + 1, :] for a in range(2)] * 2, axis=1).astype(jnp.float32)
        for d in (1, 2, 3):
            hit = ((skip[s][0] == d) & live[s][0]) | ((skip[s][1] == d) & live[s][1])
            row = jnp.where(lanes == 63 + d, jnp.where(hit, 1.0, 0.0), row)
        ext_ref[1, NEAR, 1, s:s + 1, :] = row

    def tile(i):
        return lax.rem((i + 1) // 2, 4), i % 2

    def stats(i):
        tile_stats(x_ref, *tile(i), mean_ref, rs_ref)

    def columns(i):
        tile_columns(x_ref, *tile(i), mean_ref, rs_ref, tab_ref[0:128], half_ref)

    def rows(i):
        tile_rows(*tile(i), tab_ref[640:704, 0:64], half_ref, spec_ref)

    def spectrum_copy(i):
        s, a = tile(i)
        slot = s + 2 * a
        return pltpu.make_async_remote_copy(
            src_ref=spec_ref.at[s * 2 + a], dst_ref=recv_ref.at[slot], send_sem=sem_s.at[slot], recv_sem=got_s.at[slot],
            device_id=(lax.rem(gz + nz - 1 + 2 * a, nz), xy), device_id_type=MESH)

    loads[0].wait()
    stats(0)
    loads[1].wait()
    stats(1)
    tab_load.wait()
    columns(0)
    loads[2].wait()
    loads[3].wait()
    pl.semaphore_wait(barrier, len(peers))
    early = []
    for n, (db, dx) in enumerate(close):
        early.append(pltpu.make_async_remote_copy(
            src_ref=ext_ref.at[1, NEAR], dst_ref=ext_ref.at[dx + 1, db + NEAR], send_sem=sem_e.at[n], recv_sem=got_e.at[n],
            device_id=at(-db, -dx), device_id_type=MESH))
        early[-1].start()

    def forward(i, _):
        rows(i - 2)
        columns(i - 1)
        stats(i)
        spectrum_copy(i - 2).start()
        return 0

    lax.fori_loop(2, 8, forward, 0)
    rows(6)
    columns(7)
    rows(7)

    def cross(tasks):
        pair_cross(tasks, couples, tab_ref[128:384], tab_ref[384:640], u_ref)

    def soft(step):
        pair_soft(u_ref, 2 * couples, tab_ref[640:704, 128:192], m_ref, z_ref, r_ref, step)

    def own(s, a):
        return lambda i: spec_ref[s * 2 + a, i]

    def got(slot):
        return lambda i: recv_ref[slot, i]

    def first_section(j):
        p = skip_ref[0, j]
        cross([(own(0, 0), own(p, 0)), (own(0, 1), own(p, 1))])

    def inside_block(i):
        s, p = i // 2, i - i // 4
        cross([(own(s, 0), own(p, 0)), (own(s, 1), own(p, 1))])

    def over_edge(k, m):
        cross([(own(k + 1, 0), got(m)), (got(3 + k), own(m, 1))])

    first_section(0)
    soft(0)
    first_section(1)

    def inside_step(i, _):
        soft(i - 1)
        inside_block(i)
        return 0

    lax.fori_loop(2, 5, inside_step, 0)
    for k in range(3):
        spectrum_copy(2 * k).wait_recv()
        spectrum_copy(2 * k + 1).wait_recv()
        base = 5 + k * (k + 1) // 2

        def edge_step(m, _, k=k, base=base):
            soft(base + m - 1)
            over_edge(k, m)
            return 0

        lax.fori_loop(0, k + 1, edge_step, 0)

    for c in early:
        c.wait()
    blocks = 2 * NEAR + 1
    size = 4 * blocks + 4
    here = slice(4 * NEAR, 4 * NEAR + 4)
    lane = lax.broadcasted_iota(jnp.int32, (size, 128), 1)
    col = lane % 32
    upper = (lane // 32) % 2 == 0
    inside = [jnp.where(xy > 0, 1.0, 0.0), 1.0, jnp.where(xy < nx - 1, 1.0, 0.0)]
    pad = jnp.zeros((4, 128), jnp.float32)
    weights, vel, valid_rows, live_rows = [], [], [], []
    for dx in range(3):
        info = jnp.concatenate([ext_ref[dx, k, 1] for k in range(blocks)] + [pad], axis=0)
        valid = jnp.where(lane < 64, info, pltpu.roll(info, 64, axis=1))
        on = [info[:, 64 + k:65 + k] for k in range(3)]
        weights.append([on[d - 1] * valid * shifted(valid, d) for d in (1, 2, 3)])
        vel.append(jnp.concatenate([ext_ref[dx, k, 0] for k in range(blocks)] + [pad], axis=0) * inside[dx])

    def force(fields, dx):
        v = fields[dx]
        above = fields[dx - 1] if dx > 0 else jnp.zeros_like(v)
        below = fields[dx + 1] if dx < 2 else jnp.zeros_like(v)
        lateral = jnp.where(col == 0, 0.0, pltpu.roll(v, 1, axis=1)) + jnp.where(col == 31, 0.0, pltpu.roll(v, 127, axis=1))
        down, up = pltpu.roll(v, 32, axis=1), pltpu.roll(v, 96, axis=1)
        vertical = jnp.where(upper, pltpu.roll(above, 96, axis=1) + up, down + pltpu.roll(below, 32, axis=1))
        out = STIFF * (lateral + vertical - 4.0 * v)
        for d in (1, 2, 3):
            pull = weights[dx][d - 1] * (shifted(v, d) - v)
            out += pull - shifted(pull, -d)
        return out * inside[dx]

    av = [force(vel, dx) for dx in range(3)]
    aav = force(av, 1)

    soft(STEPS - 1)
    flows = pair_finish(m_ref, z_ref, r_ref, 0, STEPS)

    for k in range(6):
        sent_ref[k:k + 1, :] = flows[5 + k]
    back = pltpu.make_async_remote_copy(
        src_ref=sent_ref, dst_ref=back_ref, send_sem=sem_b, recv_sem=got_b, device_id=at(-1, 0), device_id_type=MESH)
    back.start()

    low = (lanes // 32) % 2 == 0
    base = 4 * NEAR
    add = [[jnp.zeros((1, 128), jnp.float32) for _ in range(4)] for _ in range(3)]

    def spring(s, d):
        return weights[1][d - 1][base + s:base + s + 1]

    def push(source, target, value):
        for where, sign in ((source, -1.0), (target, 1.0)):
            add[1 + where // 4][where % 4] += sign * value

    for j in range(2):
        for d in (1, 2, 3):
            push(0, d, jnp.where(skip[0][j] == d, spring(0, d), 0.0) * flows[j])
    for i in (2, 3, 4):
        s, p = i // 2, i - i // 4
        push(s, p, spring(s, p - s) * flows[i])
    for k in range(3):
        for m in range(k + 1):
            f = flows[5 + k * (k + 1) // 2 + m]
            push(k + 1, 4 + m, jnp.where(low, spring(k + 1, 3 - k + m) * f, 0.0))
            push(k - 3, m, jnp.where(low, 0.0, spring(k - 3, 3 - k + m) * f))
    for k in range(3):
        push_ref[1, FAR, k] = jnp.concatenate(add[k], axis=0)
    late = []
    for n, (db, dx) in enumerate(wide):
        late.append(pltpu.make_async_remote_copy(
            src_ref=push_ref.at[1, FAR], dst_ref=push_ref.at[dx + 1, db + FAR], send_sem=sem_l.at[n], recv_sem=got_l.at[n],
            device_id=at(-db, -dx), device_id_type=MESH))
        late[-1].start()
    for c in late:
        c.wait_recv()
    bias = []
    for dx in range(3):
        parts = [push_ref[dx, k + 1, 1] + push_ref[dx, k, 2] + push_ref[dx, k + 2, 0] for k in range(blocks)]
        bias.append(jnp.concatenate(parts + [pad], axis=0) * inside[dx])
    ab = [force(bias, dx) for dx in range(3)]
    aab = force(ab, 1)
    basis = [x[here] for x in (vel[1], bias[1], av[1], ab[1], aav, aab)]

    index, sums = {}, []
    for i in range(6):
        for j in range(i, 6):
            index[i, j] = index[j, i] = len(sums)
            sums.append(jnp.sum(basis[i] * basis[j], axis=0, keepdims=True))
    sums = jnp.sum(jnp.concatenate(sums + [jnp.zeros((3, 128), jnp.float32)], axis=0), axis=1, keepdims=True)
    diagonal = lax.broadcasted_iota(jnp.int32, (24, 128), 0) == lax.broadcasted_iota(jnp.int32, (24, 128), 1)
    part1[0] = jnp.sum(jnp.where(diagonal, sums, 0.0), axis=0, keepdims=True)

    def scatter(part, count, peer, sem, got):
        sends = []
        for r in range(1, count):
            sends.append(pltpu.make_async_remote_copy(
                src_ref=part.at[0], dst_ref=part.at[r], send_sem=sem.at[r], recv_sem=got.at[r],
                device_id=peer(r), device_id_type=MESH))
            sends[-1].start()
        return sends

    def collect(part, sends):
        for c in sends:
            c.wait_recv()
        return functools.reduce(jnp.add, [part[r] for r in range(len(sends) + 1)])

    sends1 = scatter(part1, 4 * nx, near, sem_1, got_1)

    back.wait_recv()
    full = flows[:5] + [jnp.where(low, flows[5 + k], back_ref[k:k + 1, :]) for k in range(6)]
    step_of = {(1, 1): 2, (1, 2): 3, (2, 1): 4, (1, 3): 5, (2, 2): 6, (2, 3): 7, (3, 1): 8, (3, 2): 9, (3, 3): 10}
    for s in range(4):
        for j in range(2):
            if s == 0:
                f = full[j]
            else:
                f = jnp.where(skip[s][j] == 1, full[step_of[s, 1]], jnp.where(skip[s][j] == 2, full[step_of[s, 2]], full[step_of[s, 3]]))
            f = jnp.where(live[s][j], f, 0.0)
            for c in range(2):
                for a in range(2):
                    flow_ref[s, j, c, a:a + 1, :] = f[:, c * 64 + a * 32:c * 64 + a * 32 + 32]

    part2[0] = collect(part1, sends1)
    sends2 = scatter(part2, groups, along, sem_2, got_2)
    gram = collect(part2, sends2)
    g = {k: jnp.broadcast_to(gram[:, n:n + 1], (1, 128)) for k, n in index.items()}

    def dot(p, q):
        terms = [p[i] * q[j] * g[i, j] for i in range(6) for j in range(6) if p[i] is not None and q[j] is not None]
        return functools.reduce(jnp.add, terms)

    def plus(*xs):
        xs = [x for x in xs if x is not None]
        return functools.reduce(jnp.add, xs) if xs else None

    def times(k, x):
        return None if x is None else k * x

    one = jnp.ones((1, 128), jnp.float32)
    v = [one] + [None] * 5
    d = [None] * 6
    for it in range(ITERS):
        f = [None, one] + d[:4]
        power, speed, strength = dot(f, v), dot(v, v), dot(f, f)
        speed, strength = jnp.maximum(speed, 0.0), jnp.maximum(strength, 0.0)
        gating = 0.5 + 0.5 * power / jnp.sqrt((speed + TINY) * (strength + TINY))
        ratio = jnp.sqrt((speed + TINY) / (strength + TINY))
        mix, step = mix_ref[it], step_ref[it]
        kv, kf = gating * (1.0 - mix), gating * (mix * ratio) + step
        v = [plus(times(kv, v[i]), times(kf, f[i])) for i in range(6)]
        d = [plus(d[i], times(step, v[i])) for i in range(6)]
    result = functools.reduce(jnp.add, [d[i] * basis[i] for i in range(6)])
    for c in range(2):
        for a in range(2):
            spot = c * 64 + a * 32
            for s in range(4):
                out_ref[s, c, a:a + 1, :] = result[s:s + 1, spot:spot + 32]

    for i in range(6):
        spectrum_copy(i).wait_send()
    for c in late + [back] + sends1 + sends2:
        c.wait_send()


def body(sections, skips, patch_valid, velocity_start, step_size, mixing):
    nz, nx = lax.axis_size("gz"), lax.axis_size("xy")
    vm, sm, hbm = (pl.BlockSpec(memory_space=k) for k in (pltpu.VMEM, pltpu.SMEM, pl.ANY))
    tables = jnp.asarray(host_tables())
    width = sections.shape[2]
    couples = width // 128
    dma = pltpu.SemaphoreType.DMA
    wide = 3 * (2 * FAR + 1) - 1
    close = 3 * (2 * NEAR + 1) - 1
    f32, bf16 = jnp.float32, jnp.bfloat16
    vmem = pltpu.VMEM
    return pl.pallas_call(
        functools.partial(kernel, nz, nx),
        out_shape=(jax.ShapeDtypeStruct((4, 2, 2, 2, 32), f32), jax.ShapeDtypeStruct((4, 2, 2, 32), f32)),
        in_specs=[hbm, hbm, sm, sm, sm, vm, vm], out_specs=(vm, vm),
        scratch_shapes=[
            vmem(sections.shape, bf16), vmem(tables.shape, bf16),
            vmem((8, 1, width), f32), vmem((8, 1, width), f32),
            vmem((64, couples * 256), bf16),
            vmem((8, couples, HALF, 256), bf16), vmem((6, couples, HALF, 256), bf16),
            vmem((64, couples * 256), bf16),
            vmem((STEPS * couples * 16, 128), f32), vmem((STEPS * couples * 16, 128), f32), vmem((STEPS * couples * 16, 128), f32),
            vmem((3, 2 * NEAR + 1, 2, 4, 128), f32), vmem((3, 2 * FAR + 1, 3, 4, 128), f32),
            vmem((6, 128), f32), vmem((6, 128), f32),
            vmem((4 * nx, 1, 128), f32), vmem((nz // 4, 1, 128), f32),
            dma((4,)), dma, dma((6,)), dma((6,)), dma((close,)), dma((close,)), dma((wide,)), dma((wide,)), dma, dma,
            dma((4 * nx,)), dma((4 * nx,)), dma((nz // 4,)), dma((nz // 4,)),
        ],
        compiler_params=pltpu.CompilerParams(collective_id=0, has_side_effects=True, vmem_limit_bytes=56 * 2**20),
        name="flow_relax",
    )(sections, tables, skips, step_size, mixing, patch_valid, velocity_start)


def solution(mesh):
    in_specs = (
        P("gz", "xy", None),
        P("gz", None),
        P("gz", "xy", None),
        P("gz", None, "xy", None),
        P(),
        P(),
    )
    out_specs = (P("gz", None, None, "xy", None), P("gz", None, "xy", None))
    return jax.shard_map(body, mesh=mesh, in_specs=in_specs, out_specs=out_specs, check_vma=False)
```

time: 74.4 us -> 48.4 us (0.65)
  waiting for transfers between devices: 18 us -> 0 us
  starting transfers between devices: 3.24 us -> 0 us
  other arithmetic: 1.74 us -> 0 us
  Pallas kernels: 45.2 us -> 43.5 us
  local copies, waits for them, and re-layouts: 5.17 us -> 3.96 us
    ppermute x1 -> x0, waiting for transfers between devices: 18 us -> none  [body(): lax.ppermute(own[:REACH], 'gz', [(i, (i - 1) % nz) for i in range(nz)])]
    ppermute x1 -> x0, starting transfers between devices: 3.24 us -> none  [body(): lax.ppermute(own[:REACH], 'gz', [(i, (i - 1) % nz) for i in range(nz)])]
    concatenate x1 -> x0, other arithmetic: 1.72 us -> none  [body(): spec = jnp.concatenate([own, far], axis=0)]
    pallas_call x3 -> x1, Pallas kernels: 45.2 us -> 43.5 us  [body(): pl.pallas_call(functools.partial(kernel, nz, nx), out_shape=(jax.ShapeDty...]
    slice x1 -> x0, local copies, waits for them, and re-layouts: 1.28 us -> none  [body(): own[:REACH]]
    unnamed x26 -> x3, local copies, waits for them, and re-layouts: 3.89 us -> 3.96 us
  transfers between devices with their start and end apart: 1 -> 0, of which waited for: 1 -> 0; matrix products, arithmetic and copies ran while one was open for 0% -> 0% of each run, Pallas kernels for 0% -> 0%
where the time goes in v2:
time: 48.4 us; the launch traced here: 48.1 us
  Pallas kernels  43.5 us (90%)
  local copies, waits for them, and re-layouts  3.96 us (8%)
  between operations  0.64 us (1%)
    pallas_call x1, Pallas kernels, body(): pl.pallas_call(functools.partial(kernel, nz, nx), out_shape=(jax.ShapeDty...  43.5 us
    unnamed x3, local copies, waits for them, and re-layouts  3.96 us

profile of v2, /device:TPU:1, one launch (start us, length us, event | category | flops | bytes accessed | tf_op | source)
XLA Modules:
  0.0 48.1 jit_solution(4659991997959510531)
XLA Ops:
  0.6 1.3 %copy.9.skip_ref = s32[4,2]{1,0:T(4,128)} copy(s32[4,2]{0,1:T(2,128)} %param.8) | data formatting | bytes 64 | tf_op args[1]
  2.0 43.5 %flow_relax.1 = (f32[4,2,2,2,32]{4,3,2,1,0:T(2,128)}, f32[4,2,2,32]{3,2,1,0:T(2,128)}) custom-call(bf16[4,128,2048]{2,1,0:T(8,128)(2,1)} %x_hbm.1, bf16[704,256]{1,0:T(8,128)(2,1)} %constant.2.clone.tab_hbm, s32[4,2]{1,0:T(4,128)} %copy.9.skip_ref, f32[3]{0:T(128)} %step_ref.1, f32[3]{0:T(128)} %mix_ref.1, s32[4,2,32]{2,1,0:T(2,128)} %valid_ref.1, ...), custom_call_target="tpu_custom_call" | custom-call | tf_op jit(solution)/shard_map/flow_relax/pallas_call | solution.py:502
  45.4 1.3 %copy.12 = f32[4,2,2,2,32]{4,3,2,1,0:T(2,128)} copy(f32[4,2,2,2,32]{4,3,2,1,0:T(2,128)} %get-tuple-element.4) | data formatting | bytes 8192
  46.8 1.3 %copy.13 = f32[4,2,2,32]{3,2,1,0:T(2,128)} copy(f32[4,2,2,32]{3,2,1,0:T(2,128)} %get-tuple-element.5) | data formatting | bytes 4096

commit v3 on v2

--- a/solution.py
+++ b/solution.py
@@ -183,11 +183,20 @@
     return [u / d for u, d in zip(fold(up), fold(down))]
 
 
+def halo(reach):
+    return [(db, dx) for dx in (0, -1, 1) for db in range(-reach, reach + 1)
+            if (db, dx) != (0, 0) and abs(db) + abs(dx) <= reach]
+
+
 def shifted(x, by):
     return pltpu.roll(x, (-by) % x.shape[0], axis=0)
 
 
-def kernel(nz, nx, x_hbm, tab_hbm, skip_ref, step_ref, mix_ref, valid_ref, start_ref, flow_ref, out_ref,
+def edge_base(k):
+    return 5 + 3 * k - k * (k - 1) // 2
+
+
+def kernel(nz, nx, x_hbm, tab_hbm, skip_ref, step_ref, mix_ref, valid_ref, start_ref, out_ref,
            x_ref, tab_ref, mean_ref, rs_ref, half_ref, spec_ref, recv_ref, u_ref, m_ref, z_ref, r_ref,
            ext_ref, push_ref, back_ref, sent_ref, part1, part2,
            sem_x, sem_tab, sem_s, got_s, sem_e, got_e, sem_l, got_l, sem_b, got_b, sem_1, got_1, sem_2, got_2):
@@ -197,7 +206,16 @@
     yy, zc = gz // groups, gz % groups
     couples = spec_ref.shape[1]
 
-    loads = [pltpu.make_async_copy(x_hbm.at[s], x_ref.at[s], sem_x.at[s]) for s in range(4)]
+    def tile(i):
+        half = i // 2
+        return half + i % 2 * (3 - 2 * half), i % 2
+
+    def tile_load(i):
+        s, a = tile(i)
+        part = pl.ds(a * PATCH, PATCH)
+        return pltpu.make_async_copy(x_hbm.at[s, part], x_ref.at[s, part], sem_x.at[i])
+
+    loads = [tile_load(i) for i in range(8)]
     for c in loads:
         c.start()
     tab_load = pltpu.make_async_copy(tab_hbm, tab_ref, sem_tab)
@@ -213,15 +231,14 @@
     def along(r):
         return (yy * groups + lax.rem(zc + r, groups), xy)
 
-    wide = [(db, dx) for db in range(-FAR, FAR + 1) for dx in (-1, 0, 1) if (db, dx) != (0, 0)]
-    close = [(db, dx) for db, dx in wide if abs(db) <= NEAR]
+    wide, close = halo(FAR), halo(NEAR)
     barrier = pltpu.get_barrier_semaphore()
     peers = [at(db, dx) for db, dx in wide] + [near(r) for r in range(1, 4 * nx)] + [along(r) for r in range(1, groups)]
     for peer in peers:
         pl.semaphore_signal(barrier, inc=1, device_id=peer, device_id_type=MESH)
 
     lanes = lax.broadcasted_iota(jnp.int32, (1, 128), 1)
-    skip = [[skip_ref[s, j] for j in range(2)] for s in range(4)]
+    skip = [[skip_ref[j, s] for j in range(2)] for s in range(4)]
     live = [[(k > 0) & (gz * 4 + s + k < 4 * nz) for k in skip[s]] for s in range(4)]
     for s in range(4):
         ext_ref[1, NEAR, 0, s:s + 1, :] = jnp.concatenate(
@@ -232,9 +249,6 @@
             row = jnp.where(lanes == 63 + d, jnp.where(hit, 1.0, 0.0), row)
         ext_ref[1, NEAR, 1, s:s + 1, :] = row
 
-    def tile(i):
-        return lax.rem((i + 1) // 2, 4), i % 2
-
     def stats(i):
         tile_stats(x_ref, *tile(i), mean_ref, rs_ref)
 
@@ -257,8 +271,8 @@
     stats(1)
     tab_load.wait()
     columns(0)
-    loads[2].wait()
-    loads[3].wait()
+    for c in loads[2:]:
+        c.wait()
     pl.semaphore_wait(barrier, len(peers))
     early = []
     for n, (db, dx) in enumerate(close):
@@ -292,15 +306,15 @@
         return lambda i: recv_ref[slot, i]
 
     def first_section(j):
-        p = skip_ref[0, j]
+        p = skip_ref[j, 0]
         cross([(own(0, 0), own(p, 0)), (own(0, 1), own(p, 1))])
 
     def inside_block(i):
         s, p = i // 2, i - i // 4
         cross([(own(s, 0), own(p, 0)), (own(s, 1), own(p, 1))])
 
-    def over_edge(k, m):
-        cross([(own(k + 1, 0), got(m)), (got(3 + k), own(m, 1))])
+    def over_edge(k, q):
+        cross([(own(k + 1 + q, 0), got(k)), (got(5 - k), own(q, 1))])
 
     first_section(0)
     soft(0)
@@ -315,17 +329,16 @@
     for k in range(3):
         spectrum_copy(2 * k).wait_recv()
         spectrum_copy(2 * k + 1).wait_recv()
-        base = 5 + k * (k + 1) // 2
-
-        def edge_step(m, _, k=k, base=base):
-            soft(base + m - 1)
-            over_edge(k, m)
+
+        def edge_step(q, _, k=k):
+            soft(edge_base(k) + q - 1)
+            over_edge(k, q)
             return 0
 
-        lax.fori_loop(0, k + 1, edge_step, 0)
+        lax.fori_loop(0, 3 - k, edge_step, 0)
 
     for c in early:
-        c.wait()
+        c.wait_recv()
     blocks = 2 * NEAR + 1
     size = 4 * blocks + 4
     here = slice(4 * NEAR, 4 * NEAR + 4)
@@ -334,13 +347,61 @@
     upper = (lane // 32) % 2 == 0
     inside = [jnp.where(xy > 0, 1.0, 0.0), 1.0, jnp.where(xy < nx - 1, 1.0, 0.0)]
     pad = jnp.zeros((4, 128), jnp.float32)
-    weights, vel, valid_rows, live_rows = [], [], [], []
-    for dx in range(3):
-        info = jnp.concatenate([ext_ref[dx, k, 1] for k in range(blocks)] + [pad], axis=0)
+
+    def reaches(dx, k):
+        return abs(k - NEAR) + abs(dx - 1) <= NEAR
+
+    def gather(dx, f):
+        return jnp.concatenate([ext_ref[dx, k, f] if reaches(dx, k) else pad for k in range(blocks)] + [pad], axis=0)
+
+    def springs(dx):
+        info = gather(dx, 1)
         valid = jnp.where(lane < 64, info, pltpu.roll(info, 64, axis=1))
-        on = [info[:, 64 + k:65 + k] for k in range(3)]
-        weights.append([on[d - 1] * valid * shifted(valid, d) for d in (1, 2, 3)])
-        vel.append(jnp.concatenate([ext_ref[dx, k, 0] for k in range(blocks)] + [pad], axis=0) * inside[dx])
+        return [info[:, 63 + d:64 + d] * valid * shifted(valid, d) for d in (1, 2, 3)]
+
+    weights = [None, springs(1), None]
+    soft(STEPS - 1)
+    flows = pair_finish(m_ref, z_ref, r_ref, 0, STEPS)
+
+    for k in range(6):
+        sent_ref[k:k + 1, :] = flows[5 + k]
+    back = pltpu.make_async_remote_copy(
+        src_ref=sent_ref, dst_ref=back_ref, send_sem=sem_b, recv_sem=got_b, device_id=at(-1, 0), device_id_type=MESH)
+    back.start()
+
+    low = (lanes // 32) % 2 == 0
+    base = 4 * NEAR
+    add = [[jnp.zeros((1, 128), jnp.float32) for _ in range(4)] for _ in range(3)]
+
+    def spring(s, d):
+        return weights[1][d - 1][base + s:base + s + 1]
+
+    def push(source, target, value):
+        for where, sign in ((source, -1.0), (target, 1.0)):
+            add[1 + where // 4][where % 4] += sign * value
+
+    for j in range(2):
+        for d in (1, 2, 3):
+            push(0, d, jnp.where(skip[0][j] == d, spring(0, d), 0.0) * flows[j])
+    for i in (2, 3, 4):
+        s, p = i // 2, i - i // 4
+        push(s, p, spring(s, p - s) * flows[i])
+    for k in range(3):
+        for q in range(3 - k):
+            f = flows[edge_base(k) + q]
+            push(k + 1 + q, 4 + k, jnp.where(low, spring(k + 1 + q, 3 - q) * f, 0.0))
+            push(-1 - k, q, jnp.where(low, 0.0, spring(-1 - k, 1 + k + q) * f))
+    for k in range(3):
+        push_ref[1, FAR, k] = jnp.concatenate(add[k], axis=0)
+    late = []
+    for n, (db, dx) in enumerate(wide):
+        late.append(pltpu.make_async_remote_copy(
+            src_ref=push_ref.at[1, FAR], dst_ref=push_ref.at[dx + 1, db + FAR], send_sem=sem_l.at[n], recv_sem=got_l.at[n],
+            device_id=at(-db, -dx), device_id_type=MESH))
+        late[-1].start()
+
+    weights = [springs(0), weights[1], springs(2)]
+    vel = [gather(dx, 0) * inside[dx] for dx in range(3)]
 
     def force(fields, dx):
         v = fields[dx]
@@ -357,51 +418,12 @@
 
     av = [force(vel, dx) for dx in range(3)]
     aav = force(av, 1)
-
-    soft(STEPS - 1)
-    flows = pair_finish(m_ref, z_ref, r_ref, 0, STEPS)
-
-    for k in range(6):
-        sent_ref[k:k + 1, :] = flows[5 + k]
-    back = pltpu.make_async_remote_copy(
-        src_ref=sent_ref, dst_ref=back_ref, send_sem=sem_b, recv_sem=got_b, device_id=at(-1, 0), device_id_type=MESH)
-    back.start()
-
-    low = (lanes // 32) % 2 == 0
-    base = 4 * NEAR
-    add = [[jnp.zeros((1, 128), jnp.float32) for _ in range(4)] for _ in range(3)]
-
-    def spring(s, d):
-        return weights[1][d - 1][base + s:base + s + 1]
-
-    def push(source, target, value):
-        for where, sign in ((source, -1.0), (target, 1.0)):
-            add[1 + where // 4][where % 4] += sign * value
-
-    for j in range(2):
-        for d in (1, 2, 3):
-            push(0, d, jnp.where(skip[0][j] == d, spring(0, d), 0.0) * flows[j])
-    for i in (2, 3, 4):
-        s, p = i // 2, i - i // 4
-        push(s, p, spring(s, p - s) * flows[i])
-    for k in range(3):
-        for m in range(k + 1):
-            f = flows[5 + k * (k + 1) // 2 + m]
-            push(k + 1, 4 + m, jnp.where(low, spring(k + 1, 3 - k + m) * f, 0.0))
-            push(k - 3, m, jnp.where(low, 0.0, spring(k - 3, 3 - k + m) * f))
-    for k in range(3):
-        push_ref[1, FAR, k] = jnp.concatenate(add[k], axis=0)
-    late = []
-    for n, (db, dx) in enumerate(wide):
-        late.append(pltpu.make_async_remote_copy(
-            src_ref=push_ref.at[1, FAR], dst_ref=push_ref.at[dx + 1, db + FAR], send_sem=sem_l.at[n], recv_sem=got_l.at[n],
-            device_id=at(-db, -dx), device_id_type=MESH))
-        late[-1].start()
     for c in late:
         c.wait_recv()
     bias = []
     for dx in range(3):
-        parts = [push_ref[dx, k + 1, 1] + push_ref[dx, k, 2] + push_ref[dx, k + 2, 0] for k in range(blocks)]
+        parts = [push_ref[dx, k + 1, 1] + push_ref[dx, k, 2] + push_ref[dx, k + 2, 0] if reaches(dx, k) else pad
+                 for k in range(blocks)]
         bias.append(jnp.concatenate(parts + [pad], axis=0) * inside[dx])
     ab = [force(bias, dx) for dx in range(3)]
     aab = force(ab, 1)
@@ -433,18 +455,23 @@
     sends1 = scatter(part1, 4 * nx, near, sem_1, got_1)
 
     back.wait_recv()
-    full = flows[:5] + [jnp.where(low, flows[5 + k], back_ref[k:k + 1, :]) for k in range(6)]
-    step_of = {(1, 1): 2, (1, 2): 3, (2, 1): 4, (1, 3): 5, (2, 2): 6, (2, 3): 7, (3, 1): 8, (3, 2): 9, (3, 3): 10}
+
+    def flow_at(s, d):
+        if s + d < 4:
+            return flows[2 * s - 1 + d if s == 1 else 4]
+        far = flows[edge_base(s + d - 4) + 3 - d]
+        row = edge_base(3 - s) + s + d - 4 - 5
+        return jnp.where(low, far, back_ref[row:row + 1, :])
+
     for s in range(4):
         for j in range(2):
             if s == 0:
-                f = full[j]
+                f = flows[j]
             else:
-                f = jnp.where(skip[s][j] == 1, full[step_of[s, 1]], jnp.where(skip[s][j] == 2, full[step_of[s, 2]], full[step_of[s, 3]]))
-            f = jnp.where(live[s][j], f, 0.0)
-            for c in range(2):
-                for a in range(2):
-                    flow_ref[s, j, c, a:a + 1, :] = f[:, c * 64 + a * 32:c * 64 + a * 32 + 32]
+                f = flow_at(s, 3)
+                for d in (1, 2):
+                    f = jnp.where(skip[s][j] == d, flow_at(s, d), f)
+            out_ref[2 * s + j:2 * s + j + 1, :] = jnp.where(live[s][j], f, 0.0)
 
     part2[0] = collect(part1, sends1)
     sends2 = scatter(part2, groups, along, sem_2, got_2)
@@ -476,16 +503,22 @@
         v = [plus(times(kv, v[i]), times(kf, f[i])) for i in range(6)]
         d = [plus(d[i], times(step, v[i])) for i in range(6)]
     result = functools.reduce(jnp.add, [d[i] * basis[i] for i in range(6)])
+    out_ref[8:12, :] = result
+
+    for i in range(6):
+        spectrum_copy(i).wait_send()
+    for c in early + late + [back] + sends1 + sends2:
+        c.wait_send()
+
+
+def unpack_kernel(packed_ref, flow_ref, displace_ref):
     for c in range(2):
         for a in range(2):
-            spot = c * 64 + a * 32
+            lanes = slice(c * 64 + a * 32, c * 64 + a * 32 + 32)
             for s in range(4):
-                out_ref[s, c, a:a + 1, :] = result[s:s + 1, spot:spot + 32]
-
-    for i in range(6):
-        spectrum_copy(i).wait_send()
-    for c in late + [back] + sends1 + sends2:
-        c.wait_send()
+                displace_ref[s, c, a:a + 1, :] = packed_ref[8 + s:9 + s, lanes]
+                for j in range(2):
+                    flow_ref[s, j, c, a:a + 1, :] = packed_ref[2 * s + j:2 * s + j + 1, lanes]
 
 
 def body(sections, skips, patch_valid, velocity_start, step_size, mixing):
@@ -495,14 +528,13 @@
     width = sections.shape[2]
     couples = width // 128
     dma = pltpu.SemaphoreType.DMA
-    wide = 3 * (2 * FAR + 1) - 1
-    close = 3 * (2 * NEAR + 1) - 1
+    wide, close = len(halo(FAR)), len(halo(NEAR))
     f32, bf16 = jnp.float32, jnp.bfloat16
     vmem = pltpu.VMEM
-    return pl.pallas_call(
+    packed = pl.pallas_call(
         functools.partial(kernel, nz, nx),
-        out_shape=(jax.ShapeDtypeStruct((4, 2, 2, 2, 32), f32), jax.ShapeDtypeStruct((4, 2, 2, 32), f32)),
-        in_specs=[hbm, hbm, sm, sm, sm, vm, vm], out_specs=(vm, vm),
+        out_shape=jax.ShapeDtypeStruct((12, 128), f32),
+        in_specs=[hbm, hbm, sm, sm, sm, vm, vm], out_specs=vm,
         scratch_shapes=[
             vmem(sections.shape, bf16), vmem(tables.shape, bf16),
             vmem((8, 1, width), f32), vmem((8, 1, width), f32),
@@ -513,12 +545,17 @@
             vmem((3, 2 * NEAR + 1, 2, 4, 128), f32), vmem((3, 2 * FAR + 1, 3, 4, 128), f32),
             vmem((6, 128), f32), vmem((6, 128), f32),
             vmem((4 * nx, 1, 128), f32), vmem((nz // 4, 1, 128), f32),
-            dma((4,)), dma, dma((6,)), dma((6,)), dma((close,)), dma((close,)), dma((wide,)), dma((wide,)), dma, dma,
+            dma((8,)), dma, dma((6,)), dma((6,)), dma((close,)), dma((close,)), dma((wide,)), dma((wide,)), dma, dma,
             dma((4 * nx,)), dma((4 * nx,)), dma((nz // 4,)), dma((nz // 4,)),
         ],
         compiler_params=pltpu.CompilerParams(collective_id=0, has_side_effects=True, vmem_limit_bytes=56 * 2**20),
         name="flow_relax",
-    )(sections, tables, skips, step_size, mixing, patch_valid, velocity_start)
+    )(sections, tables, skips.T, step_size, mixing, patch_valid, velocity_start)
+    return pl.pallas_call(
+        unpack_kernel,
+        out_shape=(jax.ShapeDtypeStruct((4, 2, 2, 2, 32), f32), jax.ShapeDtypeStruct((4, 2, 2, 32), f32)),
+        in_specs=[vm], out_specs=(vm, vm), name="unpack",
+    )(packed)
 
 
 def solution(mesh):

time: 48.4 us -> 44.1 us (0.911)
  local copies, waits for them, and re-layouts: 3.96 us -> 0 us
    unnamed x3 -> x0, local copies, waits for them, and re-layouts: 3.96 us -> none
    pallas_call x1 -> x2, Pallas kernels: 43.5 us -> 43.2 us  [the longest x1 41.8 us: body(): pl.pallas_call(functools.partial(kernel, nz, nx), out_shape=jax.ShapeDtyp...]
where the time goes in v3:
time: 44.1 us; the launch traced here: 43.9 us
  Pallas kernels  43.2 us (98%)
  between operations  0.64 us (1%)
    pallas_call x1, Pallas kernels, body(): pl.pallas_call(functools.partial(kernel, nz, nx), out_shape=jax.ShapeDtyp...  41.8 us
    pallas_call x1, Pallas kernels, body(): pl.pallas_call(unpack_kernel, out_shape=(jax.ShapeDtypeStruct((4, 2, 2, 2...  1.41 us

profile of v3, /device:TPU:1, one launch (start us, length us, event | category | flops | bytes accessed | tf_op | source)
XLA Modules:
  0.0 43.9 jit_solution(16144677517623323493)
XLA Ops:
  0.6 41.8 %flow_relax.1.packed_ref = f32[12,128]{1,0:T(8,128)} custom-call(bf16[4,128,2048]{2,1,0:T(8,128)(2,1)} %x_hbm.1, bf16[704,256]{1,0:T(8,128)(2,1)} %constant.2.clone.tab_hbm, s32[2,4]{1,0:T(2,128)} %bitcast.1, f32[3]{0:T(128)} %step_ref.1, f32[3]{0:T(128)} %mix_ref.1, s32[4,2,32]{2,1,0:T(2,128)} %valid_ref.1, f32[4,2,2,32]{3,2,1,0:T(2,128)} %start_ref.1), custom_call_target="tpu_custom_call" | custom-call | tf_op jit(solution)/shard_map/flow_relax/pallas_call | solution.py:534
  42.5 1.4 %unpack.1 = (f32[4,2,2,2,32]{4,3,2,1,0:T(2,128)}, f32[4,2,2,32]{3,2,1,0:T(2,128)}) custom-call(f32[12,128]{1,0:T(8,128)} %flow_relax.1.packed_ref), custom_call_target="tpu_custom_call" | custom-call | tf_op jit(solution)/shard_map/unpack/pallas_call | solution.py:554

commit v4 on v3

--- a/solution.py
+++ b/solution.py
@@ -161,13 +161,16 @@
     a = jnp.max(jnp.where(left, top, -jnp.inf), axis=1, keepdims=True)
     b = jnp.max(jnp.where(left, -jnp.inf, top), axis=1, keepdims=True)
     peak = jnp.where(left, a, b)
-    total = jnp.zeros((rows, 128), jnp.float32)
-    along = jnp.zeros((rows, 128), jnp.float32)
-    for r in range(8):
+    beyond = jnp.zeros((rows, 128), jnp.float32)
+    stairs = jnp.zeros((rows, 128), jnp.float32)
+    eights = jnp.zeros((rows, 128), jnp.float32)
+    for r in range(7, -1, -1):
         w = jnp.exp2((pick(m_ref, r) - peak) * SCORE_EXP)
-        z = pick(z_ref, r)
-        total += w * z
-        along += w * (8.0 * pick(r_ref, r) + float(r) * z)
+        beyond += w * pick(z_ref, r)
+        eights += w * pick(r_ref, r)
+        if r > 0:
+            stairs += beyond
+    total, along = beyond, 8.0 * eights + stairs
     across = total * shift
 
     def sides(v):
@@ -196,10 +199,10 @@
     return 5 + 3 * k - k * (k - 1) // 2
 
 
-def kernel(nz, nx, x_hbm, tab_hbm, skip_ref, step_ref, mix_ref, valid_ref, start_ref, out_ref,
-           x_ref, tab_ref, mean_ref, rs_ref, half_ref, spec_ref, recv_ref, u_ref, m_ref, z_ref, r_ref,
-           ext_ref, push_ref, back_ref, sent_ref, part1, part2,
-           sem_x, sem_tab, sem_s, got_s, sem_e, got_e, sem_l, got_l, sem_b, got_b, sem_1, got_1, sem_2, got_2):
+def kernel(nz, nx, x_hbm, tab_hbm, skip_hbm, step_hbm, mix_hbm, valid_hbm, start_hbm, out_ref,
+           skip_ref, step_ref, mix_ref, valid_ref, start_ref, x_ref, tab_ref, mean_ref, rs_ref, half_ref, spec_ref, recv_ref, u_ref, m_ref, z_ref, r_ref,
+           u2_ref, ext_ref, push_ref, back_ref, sent_ref, part1, part2,
+           sem_in, sem_x, sem_tab, sem_s, got_s, sem_e, got_e, sem_l, got_l, sem_b, got_b, sem_1, got_1, sem_2, got_2, known):
     gz = lax.axis_index("gz")
     xy = lax.axis_index("xy")
     groups = nz // 4
@@ -216,7 +219,10 @@
         return pltpu.make_async_copy(x_hbm.at[s, part], x_ref.at[s, part], sem_x.at[i])
 
     loads = [tile_load(i) for i in range(8)]
-    for c in loads:
+    loads[0].start()
+    small = [(skip_hbm, skip_ref), (valid_hbm, valid_ref), (start_hbm, start_ref), (step_hbm, step_ref), (mix_hbm, mix_ref)]
+    small = [pltpu.make_async_copy(a, b, sem_in.at[n]) for n, (a, b) in enumerate(small)]
+    for c in small + loads[1:]:
         c.start()
     tab_load = pltpu.make_async_copy(tab_hbm, tab_ref, sem_tab)
     tab_load.start()
@@ -233,10 +239,18 @@
 
     wide, close = halo(FAR), halo(NEAR)
     barrier = pltpu.get_barrier_semaphore()
-    peers = [at(db, dx) for db, dx in wide] + [near(r) for r in range(1, 4 * nx)] + [along(r) for r in range(1, groups)]
+    def plane(dx, dy):
+        return (lax.rem(yy + dy + 4, 4) * groups + zc, lax.rem(xy + dx + nx, nx))
+
+    corners = [plane(dx, dy) for dx in (-1, 1) for dy in (-1, 1)]
+    ends = [along(r) for r in (4, groups - 4)]
+    peers = [at(db, dx) for db, dx in wide] + corners + [plane(0, -1), plane(0, 1)]
+    peers += [along(r) for k in range(1, 5) for r in (k, groups - k)]
     for peer in peers:
         pl.semaphore_signal(barrier, inc=1, device_id=peer, device_id_type=MESH)
 
+    for c in small:
+        c.wait()
     lanes = lax.broadcasted_iota(jnp.int32, (1, 128), 1)
     skip = [[skip_ref[j, s] for j in range(2)] for s in range(4)]
     live = [[(k > 0) & (gz * 4 + s + k < 4 * nz) for k in skip[s]] for s in range(4)]
@@ -274,6 +288,8 @@
     for c in loads[2:]:
         c.wait()
     pl.semaphore_wait(barrier, len(peers))
+    for peer in corners + ends:
+        pl.semaphore_signal(known, inc=1, device_id=peer, device_id_type=MESH)
     early = []
     for n, (db, dx) in enumerate(close):
         early.append(pltpu.make_async_remote_copy(
@@ -293,11 +309,11 @@
     columns(7)
     rows(7)
 
-    def cross(tasks):
-        pair_cross(tasks, couples, tab_ref[128:384], tab_ref[384:640], u_ref)
+    def cross(step, tasks):
+        pair_cross(tasks, couples, tab_ref[128:384], tab_ref[384:640], (u_ref, u2_ref)[step % 2])
 
     def soft(step):
-        pair_soft(u_ref, 2 * couples, tab_ref[640:704, 128:192], m_ref, z_ref, r_ref, step)
+        pair_soft((u_ref, u2_ref)[step % 2], 2 * couples, tab_ref[640:704, 128:192], m_ref, z_ref, r_ref, step)
 
     def own(s, a):
         return lambda i: spec_ref[s * 2 + a, i]
@@ -307,14 +323,14 @@
 
     def first_section(j):
         p = skip_ref[j, 0]
-        cross([(own(0, 0), own(p, 0)), (own(0, 1), own(p, 1))])
+        cross(j, [(own(0, 0), own(p, 0)), (own(0, 1), own(p, 1))])
 
     def inside_block(i):
         s, p = i // 2, i - i // 4
-        cross([(own(s, 0), own(p, 0)), (own(s, 1), own(p, 1))])
+        cross(i, [(own(s, 0), own(p, 0)), (own(s, 1), own(p, 1))])
 
     def over_edge(k, q):
-        cross([(own(k + 1 + q, 0), got(k)), (got(5 - k), own(q, 1))])
+        cross(edge_base(k) + q, [(own(k + 1 + q, 0), got(k)), (got(5 - k), own(q, 1))])
 
     first_section(0)
     soft(0)
@@ -325,8 +341,9 @@
         inside_block(i)
         return 0
 
-    lax.fori_loop(2, 5, inside_step, 0)
-    for k in range(3):
+    for i in range(2, 5):
+        inside_step(i, 0)
+    for k in range(2):
         spectrum_copy(2 * k).wait_recv()
         spectrum_copy(2 * k + 1).wait_recv()
 
@@ -335,7 +352,8 @@
             over_edge(k, q)
             return 0
 
-        lax.fori_loop(0, 3 - k, edge_step, 0)
+        for q in range(3 - k):
+            edge_step(q, 0)
 
     for c in early:
         c.wait_recv()
@@ -360,14 +378,8 @@
         return [info[:, 63 + d:64 + d] * valid * shifted(valid, d) for d in (1, 2, 3)]
 
     weights = [None, springs(1), None]
-    soft(STEPS - 1)
-    flows = pair_finish(m_ref, z_ref, r_ref, 0, STEPS)
-
-    for k in range(6):
-        sent_ref[k:k + 1, :] = flows[5 + k]
-    back = pltpu.make_async_remote_copy(
-        src_ref=sent_ref, dst_ref=back_ref, send_sem=sem_b, recv_sem=got_b, device_id=at(-1, 0), device_id_type=MESH)
-    back.start()
+    soft(STEPS - 2)
+    flows = pair_finish(m_ref, z_ref, r_ref, 0, STEPS - 1)
 
     low = (lanes // 32) % 2 == 0
     base = 4 * NEAR
@@ -386,19 +398,40 @@
     for i in (2, 3, 4):
         s, p = i // 2, i - i // 4
         push(s, p, spring(s, p - s) * flows[i])
-    for k in range(3):
+    def push_edge(k, q):
+        f = flows[edge_base(k) + q]
+        push(k + 1 + q, 4 + k, jnp.where(low, spring(k + 1 + q, 3 - q) * f, 0.0))
+        push(-1 - k, q, jnp.where(low, 0.0, spring(-1 - k, 1 + k + q) * f))
+
+    for k in range(2):
         for q in range(3 - k):
-            f = flows[edge_base(k) + q]
-            push(k + 1 + q, 4 + k, jnp.where(low, spring(k + 1 + q, 3 - q) * f, 0.0))
-            push(-1 - k, q, jnp.where(low, 0.0, spring(-1 - k, 1 + k + q) * f))
+            push_edge(k, q)
+
+    spectrum_copy(4).wait_recv()
+    spectrum_copy(5).wait_recv()
+    over_edge(2, 0)
+    soft(STEPS - 1)
+    flows += pair_finish(m_ref, z_ref, r_ref, STEPS - 1, 1)
+    push_edge(2, 0)
+
     for k in range(3):
         push_ref[1, FAR, k] = jnp.concatenate(add[k], axis=0)
     late = []
     for n, (db, dx) in enumerate(wide):
+        reach = abs(db) + abs(dx)
+        low_part = 0 if db > 0 or reach < 2 else (1 if reach < 3 else 2)
+        high_part = 3 if db < 0 or reach < 2 else (2 if reach < 3 else 1)
+        part = pl.ds(low_part, high_part - low_part)
         late.append(pltpu.make_async_remote_copy(
-            src_ref=push_ref.at[1, FAR], dst_ref=push_ref.at[dx + 1, db + FAR], send_sem=sem_l.at[n], recv_sem=got_l.at[n],
-            device_id=at(-db, -dx), device_id_type=MESH))
+            src_ref=push_ref.at[1, FAR, part], dst_ref=push_ref.at[dx + 1, db + FAR, part],
+            send_sem=sem_l.at[n], recv_sem=got_l.at[n], device_id=at(-db, -dx), device_id_type=MESH))
         late[-1].start()
+
+    for k in range(6):
+        sent_ref[k:k + 1, :] = flows[5 + k]
+    back = pltpu.make_async_remote_copy(
+        src_ref=sent_ref, dst_ref=back_ref, send_sem=sem_b, recv_sem=got_b, device_id=at(-1, 0), device_id_type=MESH)
+    back.start()
 
     weights = [springs(0), weights[1], springs(2)]
     vel = [gather(dx, 0) * inside[dx] for dx in range(3)]
@@ -452,6 +485,7 @@
             c.wait_recv()
         return functools.reduce(jnp.add, [part[r] for r in range(len(sends) + 1)])
 
+    pl.semaphore_wait(known, len(corners + ends))
     sends1 = scatter(part1, 4 * nx, near, sem_1, got_1)
 
     back.wait_recv()
@@ -473,6 +507,10 @@
                     f = jnp.where(skip[s][j] == d, flow_at(s, d), f)
             out_ref[2 * s + j:2 * s + j + 1, :] = jnp.where(live[s][j], f, 0.0)
 
+    for i in range(6):
+        spectrum_copy(i).wait_send()
+    for c in early + late + [back]:
+        c.wait_send()
     part2[0] = collect(part1, sends1)
     sends2 = scatter(part2, groups, along, sem_2, got_2)
     gram = collect(part2, sends2)
@@ -505,9 +543,7 @@
     result = functools.reduce(jnp.add, [d[i] * basis[i] for i in range(6)])
     out_ref[8:12, :] = result
 
-    for i in range(6):
-        spectrum_copy(i).wait_send()
-    for c in early + late + [back] + sends1 + sends2:
+    for c in sends1 + sends2:
         c.wait_send()
 
 
@@ -523,7 +559,7 @@
 
 def body(sections, skips, patch_valid, velocity_start, step_size, mixing):
     nz, nx = lax.axis_size("gz"), lax.axis_size("xy")
-    vm, sm, hbm = (pl.BlockSpec(memory_space=k) for k in (pltpu.VMEM, pltpu.SMEM, pl.ANY))
+    vm, hbm = (pl.BlockSpec(memory_space=k) for k in (pltpu.VMEM, pl.ANY))
     tables = jnp.asarray(host_tables())
     width = sections.shape[2]
     couples = width // 128
@@ -534,19 +570,23 @@
     packed = pl.pallas_call(
         functools.partial(kernel, nz, nx),
         out_shape=jax.ShapeDtypeStruct((12, 128), f32),
-        in_specs=[hbm, hbm, sm, sm, sm, vm, vm], out_specs=vm,
+        in_specs=[hbm] * 7, out_specs=vm,
         scratch_shapes=[
+            pltpu.SMEM((2, 4), jnp.int32), pltpu.SMEM((3,), f32), pltpu.SMEM((3,), f32),
+            vmem(patch_valid.shape, jnp.int32), vmem(velocity_start.shape, f32),
             vmem(sections.shape, bf16), vmem(tables.shape, bf16),
             vmem((8, 1, width), f32), vmem((8, 1, width), f32),
             vmem((64, couples * 256), bf16),
             vmem((8, couples, HALF, 256), bf16), vmem((6, couples, HALF, 256), bf16),
             vmem((64, couples * 256), bf16),
             vmem((STEPS * couples * 16, 128), f32), vmem((STEPS * couples * 16, 128), f32), vmem((STEPS * couples * 16, 128), f32),
+            vmem((64, couples * 256), bf16),
             vmem((3, 2 * NEAR + 1, 2, 4, 128), f32), vmem((3, 2 * FAR + 1, 3, 4, 128), f32),
             vmem((6, 128), f32), vmem((6, 128), f32),
             vmem((4 * nx, 1, 128), f32), vmem((nz // 4, 1, 128), f32),
-            dma((8,)), dma, dma((6,)), dma((6,)), dma((close,)), dma((close,)), dma((wide,)), dma((wide,)), dma, dma,
+            dma((5,)), dma((8,)), dma, dma((6,)), dma((6,)), dma((close,)), dma((close,)), dma((wide,)), dma((wide,)), dma, dma,
             dma((4 * nx,)), dma((4 * nx,)), dma((nz // 4,)), dma((nz // 4,)),
+            pltpu.SemaphoreType.REGULAR,
         ],
         compiler_params=pltpu.CompilerParams(collective_id=0, has_side_effects=True, vmem_limit_bytes=56 * 2**20),
         name="flow_relax",

time: 44.1 us -> 41.1 us (0.932)
  Pallas kernels: 43.2 us -> 40.3 us
    pallas_call x1, Pallas kernels: 41.8 us -> 38.9 us  [body(): pl.pallas_call(functools.partial(kernel, nz, nx), out_shape=jax.ShapeDtyp...]
where the time goes in v4:
time: 41.1 us; the launch traced here: 40.9 us
  Pallas kernels  40.3 us (98%)
  between operations  0.64 us (2%)
    pallas_call x1, Pallas kernels, body(): pl.pallas_call(functools.partial(kernel, nz, nx), out_shape=jax.ShapeDtyp...  38.9 us
    pallas_call x1, Pallas kernels, body(): pl.pallas_call(unpack_kernel, out_shape=(jax.ShapeDtypeStruct((4, 2, 2, 2...  1.41 us

profile of v4, /device:TPU:1, one launch (start us, length us, event | category | flops | bytes accessed | tf_op | source)
XLA Modules:
  0.0 40.9 jit_solution(15834810306215367159)
XLA Ops:
  0.6 38.9 %flow_relax.1.packed_ref = f32[12,128]{1,0:T(8,128)} custom-call(bf16[4,128,2048]{2,1,0:T(8,128)(2,1)} %x_hbm.1, bf16[704,256]{1,0:T(8,128)(2,1)} %constant.2.clone.tab_hbm, s32[2,4]{1,0:T(2,128)} %bitcast.1, f32[3]{0:T(128)} %step_hbm.1, f32[3]{0:T(128)} %mix_hbm.1, s32[4,2,32]{2,1,0:T(2,128)} %valid_hbm.1, f32[4,2,2,32]{3,2,1,0:T(2,128)} %start_hbm.1), custom_call_target="tpu_custom_call" | custom-call | tf_op jit(solution)/shard_map/flow_relax/pallas_call | solution.py:570
  39.5 1.4 %unpack.1 = (f32[4,2,2,2,32]{4,3,2,1,0:T(2,128)}, f32[4,2,2,32]{3,2,1,0:T(2,128)}) custom-call(f32[12,128]{1,0:T(8,128)} %flow_relax.1.packed_ref), custom_call_target="tpu_custom_call" | custom-call | tf_op jit(solution)/shard_map/unpack/pallas_call | solution.py:594

commit v5 on v4

--- a/solution.py
+++ b/solution.py
@@ -17,7 +17,22 @@
 LOG2E = 1.4426950408889634
 SCORE_EXP = SHARP / float(PATCH**4) * LOG2E
 MESH = pl.DeviceIdType.MESH
-STEPS = 11
+EARLY = 5
+STEPS = [
+    [(0, 0, "s0"), (1, 0, "s0")],
+    [(0, 0, "s1"), (1, 0, "s1")],
+    [(1, 1, 1), (1, 1, 2)],
+    [(0, 1, "s0"), (1, 2, 1)],
+    [(0, 1, "s1"), (2, 3, 1)],
+    [(0, 3, 1), (2, 3, 2)],
+    [(0, 2, "s0"), (2, 3, 3)],
+    [(0, 2, "s1"), (2, 2, 2)],
+    [(0, 3, 2), (2, 2, 3)],
+    [(0, 3, 3), (2, 1, 3)],
+]
+ARRIVALS = [3, 6, 9]
+SEND = 2
+SPRINGS_BACK = [(3, 1), (3, 2), (3, 3), (2, 2), (2, 3), (1, 3)]
 NEAR, FAR = 2, 3
 
 
@@ -195,10 +210,6 @@
     return pltpu.roll(x, (-by) % x.shape[0], axis=0)
 
 
-def edge_base(k):
-    return 5 + 3 * k - k * (k - 1) // 2
-
-
 def kernel(nz, nx, x_hbm, tab_hbm, skip_hbm, step_hbm, mix_hbm, valid_hbm, start_hbm, out_ref,
            skip_ref, step_ref, mix_ref, valid_ref, start_ref, x_ref, tab_ref, mean_ref, rs_ref, half_ref, spec_ref, recv_ref, u_ref, m_ref, z_ref, r_ref,
            u2_ref, ext_ref, push_ref, back_ref, sent_ref, part1, part2,
@@ -281,13 +292,16 @@
 
     loads[0].wait()
     stats(0)
+    tab_load.wait()
+    columns(0)
+    rows(0)
+    pl.semaphore_wait(barrier, len(peers))
+    spectrum_copy(0).start()
     loads[1].wait()
     stats(1)
-    tab_load.wait()
-    columns(0)
-    for c in loads[2:]:
-        c.wait()
-    pl.semaphore_wait(barrier, len(peers))
+    columns(1)
+    rows(1)
+    spectrum_copy(1).start()
     for peer in corners + ends:
         pl.semaphore_signal(known, inc=1, device_id=peer, device_id_type=MESH)
     early = []
@@ -296,64 +310,65 @@
             src_ref=ext_ref.at[1, NEAR], dst_ref=ext_ref.at[dx + 1, db + NEAR], send_sem=sem_e.at[n], recv_sem=got_e.at[n],
             device_id=at(-db, -dx), device_id_type=MESH))
         early[-1].start()
+    for c in loads[2:]:
+        c.wait()
+    stats(2)
+    stats(3)
+    columns(2)
 
     def forward(i, _):
         rows(i - 2)
         columns(i - 1)
         stats(i)
-        spectrum_copy(i - 2).start()
         return 0
 
-    lax.fori_loop(2, 8, forward, 0)
+    lax.fori_loop(4, 8, forward, 0)
+    spectrum_copy(2).start()
+    spectrum_copy(3).start()
     rows(6)
     columns(7)
     rows(7)
 
-    def cross(step, tasks):
-        pair_cross(tasks, couples, tab_ref[128:384], tab_ref[384:640], (u_ref, u2_ref)[step % 2])
+    def own(s, a):
+        return lambda i: spec_ref[s * 2 + a, i]
+
+    def got(slot):
+        return lambda i: recv_ref[slot, i]
+
+    def task(kind, s, what):
+        if kind == 2:
+            return got(2 + s), own(s + what - 4, 1)
+        if what not in ("s0", "s1"):
+            return own(s, kind), got(s + what - 4) if s + what > 3 else own(s + what, kind)
+        d = skip_ref[int(what[1]), s]
+        if s == 0:
+            return own(0, kind), own(d, kind)
+        if s == 1:
+            inner = own(jnp.minimum(d + 1, 3), kind)
+            return own(1, kind), lambda i: jnp.where(d == 3, recv_ref[0, i], inner(i))
+        return own(2, kind), lambda i: jnp.where(d == 1, spec_ref[6 + kind, i], jnp.where(d == 2, recv_ref[0, i], recv_ref[1, i]))
+
+    def cross(step):
+        pair_cross([task(*t) for t in STEPS[step]], couples, tab_ref[128:384], tab_ref[384:640], (u_ref, u2_ref)[step % 2])
 
     def soft(step):
         pair_soft((u_ref, u2_ref)[step % 2], 2 * couples, tab_ref[640:704, 128:192], m_ref, z_ref, r_ref, step)
 
-    def own(s, a):
-        return lambda i: spec_ref[s * 2 + a, i]
-
-    def got(slot):
-        return lambda i: recv_ref[slot, i]
-
-    def first_section(j):
-        p = skip_ref[j, 0]
-        cross(j, [(own(0, 0), own(p, 0)), (own(0, 1), own(p, 1))])
-
-    def inside_block(i):
-        s, p = i // 2, i - i // 4
-        cross(i, [(own(s, 0), own(p, 0)), (own(s, 1), own(p, 1))])
-
-    def over_edge(k, q):
-        cross(edge_base(k) + q, [(own(k + 1 + q, 0), got(k)), (got(5 - k), own(q, 1))])
-
-    first_section(0)
-    soft(0)
-    first_section(1)
-
-    def inside_step(i, _):
-        soft(i - 1)
-        inside_block(i)
-        return 0
-
-    for i in range(2, 5):
-        inside_step(i, 0)
-    for k in range(2):
-        spectrum_copy(2 * k).wait_recv()
-        spectrum_copy(2 * k + 1).wait_recv()
-
-        def edge_step(q, _, k=k):
-            soft(edge_base(k) + q - 1)
-            over_edge(k, q)
-            return 0
-
-        for q in range(3 - k):
-            edge_step(q, 0)
+    last = len(STEPS) - 1
+    flows = []
+    cross(0)
+    for step in range(1, last):
+        if step in ARRIVALS:
+            k = ARRIVALS.index(step)
+            spectrum_copy(2 * k).wait_recv()
+            spectrum_copy(2 * k + 1).wait_recv()
+        if step == SEND:
+            spectrum_copy(4).start()
+            spectrum_copy(5).start()
+        soft(step - 1)
+        cross(step)
+        if step == EARLY:
+            flows += pair_finish(m_ref, z_ref, r_ref, 0, EARLY)
 
     for c in early:
         c.wait_recv()
@@ -378,8 +393,8 @@
         return [info[:, 63 + d:64 + d] * valid * shifted(valid, d) for d in (1, 2, 3)]
 
     weights = [None, springs(1), None]
-    soft(STEPS - 2)
-    flows = pair_finish(m_ref, z_ref, r_ref, 0, STEPS - 1)
+    soft(last - 1)
+    flows += pair_finish(m_ref, z_ref, r_ref, EARLY, last - EARLY)
 
     low = (lanes // 32) % 2 == 0
     base = 4 * NEAR
@@ -392,27 +407,28 @@
         for where, sign in ((source, -1.0), (target, 1.0)):
             add[1 + where // 4][where % 4] += sign * value
 
-    for j in range(2):
-        for d in (1, 2, 3):
-            push(0, d, jnp.where(skip[0][j] == d, spring(0, d), 0.0) * flows[j])
-    for i in (2, 3, 4):
-        s, p = i // 2, i - i // 4
-        push(s, p, spring(s, p - s) * flows[i])
-    def push_edge(k, q):
-        f = flows[edge_base(k) + q]
-        push(k + 1 + q, 4 + k, jnp.where(low, spring(k + 1 + q, 3 - q) * f, 0.0))
-        push(-1 - k, q, jnp.where(low, 0.0, spring(-1 - k, 1 + k + q) * f))
-
-    for k in range(2):
-        for q in range(3 - k):
-            push_edge(k, q)
+    def push_step(step):
+        for slot, (kind, s, what) in enumerate(STEPS[step]):
+            f = flows[step]
+            if slot != min(kind, 1):
+                f = pltpu.roll(f, 32, axis=1)
+            f = jnp.where(low, f, 0.0) if kind == 0 else jnp.where(low, 0.0, f)
+            where = s - 4 if kind == 2 else s
+            if what in ("s0", "s1"):
+                for d in (1, 2, 3):
+                    push(where, where + d, jnp.where(skip[s][int(what[1])] == d, spring(where, d), 0.0) * f)
+            else:
+                push(where, where + what, spring(where, what) * f)
+
+    for step in range(last):
+        push_step(step)
 
     spectrum_copy(4).wait_recv()
     spectrum_copy(5).wait_recv()
-    over_edge(2, 0)
-    soft(STEPS - 1)
-    flows += pair_finish(m_ref, z_ref, r_ref, STEPS - 1, 1)
-    push_edge(2, 0)
+    cross(last)
+    soft(last)
+    flows += pair_finish(m_ref, z_ref, r_ref, last, 1)
+    push_step(last)
 
     for k in range(3):
         push_ref[1, FAR, k] = jnp.concatenate(add[k], axis=0)
@@ -427,8 +443,9 @@
             send_sem=sem_l.at[n], recv_sem=got_l.at[n], device_id=at(-db, -dx), device_id_type=MESH))
         late[-1].start()
 
-    for k in range(6):
-        sent_ref[k:k + 1, :] = flows[5 + k]
+    step_of = {t: step for step, tasks in enumerate(STEPS) for t in tasks}
+    for n, (s, d) in enumerate(SPRINGS_BACK):
+        sent_ref[n:n + 1, :] = flows[step_of[2, s, d]]
     back = pltpu.make_async_remote_copy(
         src_ref=sent_ref, dst_ref=back_ref, send_sem=sem_b, recv_sem=got_b, device_id=at(-1, 0), device_id_type=MESH)
     back.start()
@@ -469,7 +486,7 @@
             sums.append(jnp.sum(basis[i] * basis[j], axis=0, keepdims=True))
     sums = jnp.sum(jnp.concatenate(sums + [jnp.zeros((3, 128), jnp.float32)], axis=0), axis=1, keepdims=True)
     diagonal = lax.broadcasted_iota(jnp.int32, (24, 128), 0) == lax.broadcasted_iota(jnp.int32, (24, 128), 1)
-    part1[0] = jnp.sum(jnp.where(diagonal, sums, 0.0), axis=0, keepdims=True)
+    part2[0] = jnp.sum(jnp.where(diagonal, sums, 0.0), axis=0, keepdims=True)
 
     def scatter(part, count, peer, sem, got):
         sends = []
@@ -486,34 +503,36 @@
         return functools.reduce(jnp.add, [part[r] for r in range(len(sends) + 1)])
 
     pl.semaphore_wait(known, len(corners + ends))
-    sends1 = scatter(part1, 4 * nx, near, sem_1, got_1)
+    sends1 = scatter(part2, groups, along, sem_2, got_2)
 
     back.wait_recv()
 
-    def flow_at(s, d):
-        if s + d < 4:
-            return flows[2 * s - 1 + d if s == 1 else 4]
-        far = flows[edge_base(s + d - 4) + 3 - d]
-        row = edge_base(3 - s) + s + d - 4 - 5
-        return jnp.where(low, far, back_ref[row:row + 1, :])
+    def flow_at(kind, s, j):
+        if (kind, s, "s0") in step_of:
+            return flows[step_of[kind, s, f"s{j}"]]
+        rows = []
+        for d in (1, 2, 3):
+            if kind == 1 and (s, d) in SPRINGS_BACK:
+                n = SPRINGS_BACK.index((s, d))
+                rows.append(back_ref[n:n + 1, :])
+            else:
+                step = step_of[kind, s, d]
+                f = flows[step]
+                rows.append(f if STEPS[step][kind] == (kind, s, d) else pltpu.roll(f, 32, axis=1))
+        return jnp.where(skip[s][j] == 1, rows[0], jnp.where(skip[s][j] == 2, rows[1], rows[2]))
 
     for s in range(4):
         for j in range(2):
-            if s == 0:
-                f = flows[j]
-            else:
-                f = flow_at(s, 3)
-                for d in (1, 2):
-                    f = jnp.where(skip[s][j] == d, flow_at(s, d), f)
+            f = jnp.where(low, flow_at(0, s, j), flow_at(1, s, j))
             out_ref[2 * s + j:2 * s + j + 1, :] = jnp.where(live[s][j], f, 0.0)
 
     for i in range(6):
         spectrum_copy(i).wait_send()
     for c in early + late + [back]:
         c.wait_send()
-    part2[0] = collect(part1, sends1)
-    sends2 = scatter(part2, groups, along, sem_2, got_2)
-    gram = collect(part2, sends2)
+    part1[0] = collect(part2, sends1)
+    sends2 = scatter(part1, 4 * nx, near, sem_1, got_1)
+    gram = collect(part1, sends2)
     g = {k: jnp.broadcast_to(gram[:, n:n + 1], (1, 128)) for k, n in index.items()}
 
     def dot(p, q):
@@ -579,7 +598,7 @@
             vmem((64, couples * 256), bf16),
             vmem((8, couples, HALF, 256), bf16), vmem((6, couples, HALF, 256), bf16),
             vmem((64, couples * 256), bf16),
-            vmem((STEPS * couples * 16, 128), f32), vmem((STEPS * couples * 16, 128), f32), vmem((STEPS * couples * 16, 128), f32),
+            vmem((len(STEPS) * couples * 32 * 8 // 16, 128), f32), vmem((len(STEPS) * couples * 32 * 8 // 16, 128), f32), vmem((len(STEPS) * couples * 32 * 8 // 16, 128), f32),
             vmem((64, couples * 256), bf16),
             vmem((3, 2 * NEAR + 1, 2, 4, 128), f32), vmem((3, 2 * FAR + 1, 3, 4, 128), f32),
             vmem((6, 128), f32), vmem((6, 128), f32),

time: 41.1 us -> 40.2 us (0.978)
  Pallas kernels: 40.3 us -> 39.4 us
    pallas_call x1, Pallas kernels: 38.9 us -> 38 us  [body(): pl.pallas_call(functools.partial(kernel, nz, nx), out_shape=jax.ShapeDtyp...]
where the time goes in v5:
time: 40.2 us; the launch traced here: 40 us
  Pallas kernels  39.4 us (98%)
  between operations  0.64 us (2%)
    pallas_call x1, Pallas kernels, body(): pl.pallas_call(functools.partial(kernel, nz, nx), out_shape=jax.ShapeDtyp...  38 us
    pallas_call x1, Pallas kernels, body(): pl.pallas_call(unpack_kernel, out_shape=(jax.ShapeDtypeStruct((4, 2, 2, 2...  1.41 us

profile of v5, /device:TPU:1, one launch (start us, length us, event | category | flops | bytes accessed | tf_op | source)
XLA Modules:
  0.0 40.0 jit_solution(10498696478444245429)
XLA Ops:
  0.6 38.0 %flow_relax.1.packed_ref = f32[12,128]{1,0:T(8,128)} custom-call(bf16[4,128,2048]{2,1,0:T(8,128)(2,1)} %x_hbm.1, bf16[704,256]{1,0:T(8,128)(2,1)} %constant.2.clone.tab_hbm, s32[2,4]{1,0:T(2,128)} %bitcast.1, f32[3]{0:T(128)} %step_hbm.1, f32[3]{0:T(128)} %mix_hbm.1, s32[4,2,32]{2,1,0:T(2,128)} %valid_hbm.1, f32[4,2,2,32]{3,2,1,0:T(2,128)} %start_hbm.1), custom_call_target="tpu_custom_call" | custom-call | tf_op jit(solution)/shard_map/flow_relax/pallas_call | solution.py:589
  38.6 1.4 %unpack.1 = (f32[4,2,2,2,32]{4,3,2,1,0:T(2,128)}, f32[4,2,2,32]{3,2,1,0:T(2,128)}) custom-call(f32[12,128]{1,0:T(8,128)} %flow_relax.1.packed_ref), custom_call_target="tpu_custom_call" | custom-call | tf_op jit(solution)/shard_map/unpack/pallas_call | solution.py:613

commit v6 on v5

--- a/solution.py
+++ b/solution.py
@@ -222,7 +222,8 @@
 
     def tile(i):
         half = i // 2
-        return half + i % 2 * (3 - 2 * half), i % 2
+        a = 1 - i % 2
+        return half + a * (3 - 2 * half), a
 
     def tile_load(i):
         s, a = tile(i)

time: 40.2 us -> 40 us (level)
  no operation moved by 1% of the time
where the time goes in v6:
time: 40 us; the launch traced here: 39.8 us
  Pallas kernels  39.2 us (98%)
  between operations  0.64 us (2%)
    pallas_call x1, Pallas kernels, body(): pl.pallas_call(functools.partial(kernel, nz, nx), out_shape=jax.ShapeDtyp...  37.8 us
    pallas_call x1, Pallas kernels, body(): pl.pallas_call(unpack_kernel, out_shape=(jax.ShapeDtypeStruct((4, 2, 2, 2...  1.41 us

profile of v6, /device:TPU:1, one launch (start us, length us, event | category | flops | bytes accessed | tf_op | source)
XLA Modules:
  0.0 39.8 jit_solution(9504070697399234890)
XLA Ops:
  0.6 37.8 %flow_relax.1.packed_ref = f32[12,128]{1,0:T(8,128)} custom-call(bf16[4,128,2048]{2,1,0:T(8,128)(2,1)} %x_hbm.1, bf16[704,256]{1,0:T(8,128)(2,1)} %constant.2.clone.tab_hbm, s32[2,4]{1,0:T(2,128)} %bitcast.1, f32[3]{0:T(128)} %step_hbm.1, f32[3]{0:T(128)} %mix_hbm.1, s32[4,2,32]{2,1,0:T(2,128)} %valid_hbm.1, f32[4,2,2,32]{3,2,1,0:T(2,128)} %start_hbm.1), custom_call_target="tpu_custom_call" | custom-call | tf_op jit(solution)/shard_map/flow_relax/pallas_call | solution.py:590
  38.4 1.4 %unpack.1 = (f32[4,2,2,2,32]{4,3,2,1,0:T(2,128)}, f32[4,2,2,32]{3,2,1,0:T(2,128)}) custom-call(f32[12,128]{1,0:T(8,128)} %flow_relax.1.packed_ref), custom_call_target="tpu_custom_call" | custom-call | tf_op jit(solution)/shard_map/unpack/pallas_call | solution.py:614
